TPU v7x, 256 devices: a whole 4x4x8 slice. The times are simulated.
256 devices in a mesh: facet: 32 (over y_lo, z, core), half: 4 (over x), sub: 2 (over y_hi).
Axes of the slice: x: 4, y: 4 (y_hi: 2, y_lo: 2; y = y_hi * 2 + y_lo), z: 8, core: 2. Of those that a mesh axis runs over, the one named last changes fastest.
Arguments:
- facets: bfloat16 [32, 2, 2048, 2048], P('facet', None, ('half', 'sub')), may hold values from -6 to 6
- weights: float32 [512, 16, 512], P('facet', ('half', 'sub')), may hold values from 0.25 to 4
- facet_offsets: int32 [32, 2], replicated, may hold values from 0 to 511
- subgrid_offsets: int32 [16], replicated, may hold values from 0 to 2047
- column: int32 [1], replicated, may hold values from 0 to 2047
Outputs:
- facet_update: bfloat16 [32, 2, 2048, 2048], P('facet', None, ('half', 'sub'))
- spectra: float32 [512, 16, 2, 512], P('facet', ('half', 'sub'))
All inputs are finite; a program needn't handle non-finite values.
Results may differ from a plain program's by a relative error of at most 0.025.
Values may be sent and summed in bfloat16 or wider, within the bound.
A program may use at most 128 MiB of HBM per device.

v0:
```python
import math

import jax
import jax.numpy as jnp
from jax import lax
from jax.sharding import PartitionSpec as P

YF = 2048
M = 128
XM = 512


def laid_out(tiles, dim):
    lengths = list(tiles.shape[1:])
    lengths[dim] *= tiles.shape[0]
    return jnp.moveaxis(tiles, 0, dim).reshape(lengths)


def sent_to_all(value, axis):
    size = lax.axis_size(axis)
    return lax.all_to_all(
        jnp.broadcast_to(value[None], (size, *value.shape)), axis, 0, 0, tiled=True
    )


def gather_directly(value, axis, dim):
    return laid_out(sent_to_all(value, axis), dim)


def as_sent(value):

    def short(part):
        return part.astype(jnp.bfloat16) if part.dtype == jnp.float32 else part

    return jax.tree.map(short, value)


def wave(freq, pos, n):
    turns = freq[:, None] * pos[None, :] % n
    angle = turns.astype(jnp.float32) * (2.0 * math.pi / n)
    return (jnp.cos(angle), jnp.sin(angle))


def facet_table(freq, pos, n):
    cosine, sine = wave(freq, pos, n)
    shaped = (jnp.sin(math.pi * (pos.astype(jnp.float32) + 0.5) / n) ** 2)[None, :] / math.sqrt(n)
    return ((cosine * shaped).astype(jnp.bfloat16), (-sine * shaped).astype(jnp.bfloat16))


def left_apply(table, data):
    prod = jnp.einsum("pjn,nscw->pjscw", table, data)
    real = prod[0, :, :, 0] - prod[1, :, :, 1]
    imag = prod[0, :, :, 1] + prod[1, :, :, 0]
    return jnp.stack([real, imag], 2)


def right_apply(data, table):
    prod = jnp.einsum("...cn,pnw->...pcw", data, table)
    real = prod[..., 0, 0, :] - prod[..., 1, 1, :]
    imag = prod[..., 0, 1, :] + prod[..., 1, 0, :]
    return jnp.stack([real, imag], -2)


def shards(facets, weights, facet_offsets, subgrid_offsets, column):
    planes = facets[0]
    rows_here = planes.shape[1]
    block_rows = weights.shape[0]
    sub_here = weights.shape[1]
    count_facets = facet_offsets.shape[0]
    f32 = jnp.float32
    mine = lax.axis_index("facet")
    member = lax.axis_index(("half", "sub"))
    first_row = member * rows_here
    own_offset = lax.dynamic_index_in_dim(facet_offsets, mine, 0, keepdims=False)
    local_pos = first_row + jnp.arange(rows_here, dtype=jnp.int32)
    every_pos = jnp.arange(YF, dtype=jnp.int32)
    near = jnp.arange(M, dtype=jnp.int32)
    span = jnp.arange(XM, dtype=jnp.int32)
    scale = 1.0 / math.sqrt(XM)
    cos_full, sin_full = wave(span, span, XM)
    column_freq = (column[0] + near) % YF
    q_real, q_imag = facet_table(column_freq, every_pos, YF)
    q_both = jnp.concatenate([q_real, q_imag], 0)
    contract = (((1,), (1,)), ((), ()))
    from_real = lax.dot_general(planes[0], q_both, contract, preferred_element_type=f32)
    from_imag = lax.dot_general(planes[1], q_both, contract, preferred_element_type=f32)
    a_both = jnp.concatenate(
        [from_real[:, :M] - from_imag[:, M:], from_real[:, M:] + from_imag[:, :M]], 1
    ).astype(jnp.bfloat16)
    own_subs = lax.dynamic_slice_in_dim(subgrid_offsets, member * sub_here, sub_here)
    own_freq = ((own_subs[:, None] + near[None, :]) % YF).reshape(-1)
    piece = gather_directly(a_both, ("half", "sub"), 0)
    pos = jnp.arange(piece.shape[0], dtype=jnp.int32)
    p_real, p_imag = facet_table(own_freq, pos, YF)
    t_real = jnp.dot(p_real, piece, preferred_element_type=f32)
    t_imag = jnp.dot(p_imag, piece, preferred_element_type=f32)
    c_real = (t_real[:, :M] - t_imag[:, M:]).reshape(sub_here, M, M)
    c_imag = (t_real[:, M:] + t_imag[:, :M]).reshape(sub_here, M, M)
    contrib = jnp.stack([c_real, c_imag], 2)
    row_index = (own_offset[0] + near) % XM
    cos_r = jnp.take(cos_full, row_index, axis=1)
    sin_r = jnp.take(sin_full, row_index, axis=1)
    row_table = jnp.stack([cos_r, -sin_r]) * scale
    k_both = left_apply(row_table, jnp.transpose(contrib, (1, 0, 2, 3)))
    moved = lax.all_to_all(
        k_both[:, :, :, None, :].astype(jnp.bfloat16),
        "facet",
        split_axis=0,
        concat_axis=3,
        tiled=True,
    ).astype(jnp.float32)
    all_cols = ((facet_offsets[:, 1:2] + near[None, :]) % XM).reshape(-1)
    cos_c = jnp.take(cos_full, all_cols, axis=0)
    sin_c = jnp.take(sin_full, all_cols, axis=0)
    spectrum = right_apply(
        moved.reshape(block_rows, sub_here, 2, count_facets * M), jnp.stack([cos_c, -sin_c]) * scale
    )
    weighted = weights[:, :, None, :] * spectrum
    cos_w = jnp.take(cos_full, row_index, axis=0)
    sin_w = jnp.take(sin_full, row_index, axis=0)
    cos_b = jnp.take(cos_full, all_cols, axis=1)
    sin_b = jnp.take(sin_full, all_cols, axis=1)
    outgoing = right_apply(weighted, jnp.stack([cos_b, sin_b]) * scale)
    back = lax.all_to_all(
        as_sent(outgoing.reshape(block_rows, sub_here, 2, count_facets, M)),
        "facet",
        split_axis=3,
        concat_axis=0,
        tiled=True,
    )
    windows = left_apply(jnp.stack([cos_w, sin_w]) * scale, back[:, :, :, 0, :])
    windows = jnp.transpose(windows, (1, 0, 2, 3)).astype(jnp.bfloat16)
    piece = gather_directly(windows, ("half", "sub"), 0)
    count = piece.shape[0]
    freq = ((subgrid_offsets[:, None] + near[None, :]) % YF).reshape(-1)
    p_real, p_imag = facet_table(freq, local_pos, YF)
    flat = piece.reshape(count * M, 2 * M)
    over = (((0,), (0,)), ((), ()))
    t_real = lax.dot_general(p_real, flat, over, preferred_element_type=f32)
    t_imag = lax.dot_general(p_imag, flat, over, preferred_element_type=f32)
    e_both = jnp.concatenate(
        [t_real[:, :M] + t_imag[:, M:], t_real[:, M:] - t_imag[:, :M]], 1
    ).astype(jnp.bfloat16)
    u_real = jnp.dot(e_both, q_both, preferred_element_type=f32)
    u_imag = jnp.dot(e_both, jnp.concatenate([-q_imag, q_real], 0), preferred_element_type=f32)
    gain = 2.0 * math.sqrt(YF / M)
    update = (jnp.stack([u_real, u_imag]) * gain).astype(jnp.bfloat16)[None]
    return (update, weighted)


def solution(mesh):
    return jax.shard_map(
        shards,
        mesh=mesh,
        in_specs=(
            P("facet", None, ("half", "sub"), None),
            P("facet", ("half", "sub"), None),
            P(),
            P(),
            P(),
        ),
        out_specs=(
            P("facet", None, ("half", "sub"), None),
            P("facet", ("half", "sub"), None, None),
        ),
        check_vma=False,
    )
```

profile of v0, /device:TPU:1, one launch (start us, length us, event | category | flops | bytes accessed | tf_op | source)
XLA Modules:
  0.0 261.7 jit_solution(16826695247347700905)
XLA Ops:
  1.4 4.6 %multiply_convert_fusion.8 = (bf16[128,2048]{1,0:T(8,128)(2,1)S(1)}, bf16[128,2048]{1,0:T(8,128)(2,1)S(1)}) fusion(f32[2048]{0:T(1024)S(1)} %multiply_multiply_fusion, s32[128]{0:T(128)S(1)} %and_select_fusion), kind=kLoop, calls=%fused_computation.80 | loop fusion | flops 4980736 | bytes 1057280 | tf_op jit(solution)/shard_map/convert_element_type | solution.py:47
  6.0 2.1 convolution_bitcast_fusion.2
  8.1 0.2 copy-done.7
  8.2 0.5 convolution_bitcast_fusion.3
  8.8 0.1 copy.39
  8.9 1.1 broadcast_in_dim.40
  10.0 7.7 %all-to-all-start = ((bf16[8,256,256]{2,1,0:T(8,128)(2,1)}), bf16[8,256,256]{2,1,0:T(8,128)(2,1)}, u32[]{:S(2)}, u32[]{:S(2)}) async-start(bf16[8,256,256]{2,1,0:T(8,128)(2,1)} %broadcast_in_dim.40), calls=%async_computation | async-start | bytes 2097152 | tf_op jit(solution)/shard_map/all_to_all | solution.py:21
  17.7 3.8 %fusion.79 = f32[512,512]{1,0:T(8,128)S(1)} fusion(), kind=kLoop, calls=%fused_computation.117 | loop fusion | flops 3670016 | bytes 1048576 | tf_op jit(solution)/shard_map/sin | solution.py:41
  21.5 3.8 %fusion.80 = f32[512,512]{1,0:T(8,128)S(1)} fusion(), kind=kLoop, calls=%fused_computation.118 | loop fusion | flops 3670016 | bytes 1048576 | tf_op jit(solution)/shard_map/cos | solution.py:41
  25.3 0.3 copy.32
  25.7 1.3 copy.30
  27.0 0.1 broadcast_clamp_fusion
  27.1 16.7 %gather_fusion.4 = f32[4096,512]{1,0:T(8,128)} fusion(f32[512,512]{1,0:T(8,128)S(1)} %fusion.80, s32[4096]{0:T(1024)S(1)} %broadcast_clamp_fusion), kind=kCustom, calls=%fused_computation.2.clone | custom fusion | bytes 16793600 | tf_op jit(solution)/shard_map/jit(_take)/gather | solution.py:113
  43.8 16.7 %gather_fusion.5 = f32[4096,512]{1,0:T(8,128)} fusion(f32[512,512]{1,0:T(8,128)S(1)} %fusion.79, s32[4096]{0:T(1024)S(1)} %broadcast_clamp_fusion), kind=kCustom, calls=%fused_computation.6.clone | custom fusion | bytes 16793600 | tf_op jit(solution)/shard_map/jit(_take)/gather | solution.py:114
  60.5 0.1 compare_and_fusion
  60.6 0.1 constant_dynamic-slice_fusion
  60.7 0.5 slice.99
  61.2 0.7 compare_select_fusion.1
  61.9 19.2 %gather_fusion.2 = f32[4096,512]{1,0:T(8,128)} fusion(f32[512,512]{0,1:T(8,128)} %copy.30, s32[4096]{0:T(1024)S(1)} %broadcast_clamp_fusion), kind=kCustom, calls=%fused_computation.1.clone | custom fusion | bytes 16793600 | tf_op jit(solution)/shard_map/jit(_take)/gather | solution.py:121
  81.0 11.4 %select_bitcast_fusion = (f32[1,4096,512]{2,1,0:T(8,128)}, f32[1,4096,512]{2,1,0:T(8,128)}) fusion(f32[4096,512]{1,0:T(8,128)} %gather_fusion.4, pred[4096]{0:T(1024)(128)(4,1)S(1)} %compare_and_fusion, f32[4096,512]{1,0:T(8,128)} %gather_fusion.5), kind=kLoop, calls=%fused_computation.20 | loop fusion | flops 6291456 | bytes 33558528 | tf_op jit(solution)/shard_map/stack | solution.py:116
  92.4 2.1 gather_fusion.6
  94.5 1.5 gather_fusion.7
  96.0 16.7 %gather_fusion.3 = f32[4096,512]{1,0:T(8,128)} fusion(f32[512,512]{0,1:T(8,128)S(1)} %copy.32, s32[4096]{0:T(1024)S(1)} %broadcast_clamp_fusion), kind=kCustom, calls=%fused_computation.5.clone | custom fusion | bytes 16793600 | tf_op jit(solution)/shard_map/jit(_take)/gather | solution.py:122
  112.7 1.1 copy.38
  113.8 0.1 copy.36
  114.0 8.9 %copy.31 = f32[4096,512]{0,1:T(8,128)} copy(f32[4096,512]{1,0:T(8,128)} %gather_fusion.2) | data formatting | bytes 16777216 | tf_op jit(solution)/shard_map/jit(_take)/gather | solution.py:121
  122.9 9.3 %copy.33 = f32[4096,512]{0,1:T(8,128)} copy(f32[4096,512]{1,0:T(8,128)} %gather_fusion.3) | data formatting | bytes 16777216 | tf_op jit(solution)/shard_map/jit(_take)/gather | solution.py:122
  132.3 0.1 dynamic_slice.8
  132.3 0.7 compare_and_fusion.1
  133.0 0.1 and_select_fusion.1
  133.1 9.2 %fusion.36 = f32[256,256]{1,0:T(8,128)S(1)} fusion(bf16[2048,256]{1,0:T(8,128)(2,1)} %bitcast.30, f32[2048]{0:T(1024)S(1)} %multiply_multiply_fusion, s32[256]{0:T(256)S(1)} %and_select_fusion.1), kind=kOutput, calls=%fused_computation.67 | convolution fusion | flops 276824064 | bytes 1319936 | tf_op jit(solution)/shard_map/dot_general | solution.py:95
  142.3 9.5 %fusion.37 = f32[256,256]{1,0:T(8,128)S(1)} fusion(bf16[2048,256]{1,0:T(8,128)(2,1)} %bitcast.30, f32[2048]{0:T(1024)S(1)} %multiply_multiply_fusion, s32[256]{0:T(256)S(1)} %and_select_fusion.1), kind=kOutput, calls=%fused_computation.68 | convolution fusion | flops 277348352 | bytes 1319936 | tf_op jit(solution)/shard_map/dot_general | solution.py:96
  151.8 0.4 fusion.75
  152.3 0.1 fusion.82
  152.4 1.3 copy.44
  153.8 9.7 %all-to-all-start.1 = ((bf16[512,2,2,1,128]{4,1,3,2,0:T(2,128)(2,1)}), bf16[512,2,2,1,128]{4,1,3,2,0:T(2,128)(2,1)S(1)}, u32[]{:S(2)}, u32[]{:S(2)}) async-start(bf16[512,2,2,1,128]{4,1,3,2,0:T(2,128)(2,1)} %copy.44), calls=%async_computation.1 | async-start | bytes 1048576 | tf_op jit(solution)/shard_map/all_to_all | solution.py:105
  163.5 10.9 %select_bitcast_fusion.2 = (f32[1,512,4096]{2,1,0:T(8,128)}, f32[1,512,4096]{2,1,0:T(8,128)}) fusion(f32[4096,512]{0,1:T(8,128)} %copy.31, pred[4096]{0:T(1024)(128)(4,1)S(1)} %compare_and_fusion, f32[4096,512]{0,1:T(8,128)} %copy.33), kind=kLoop, calls=%fused_computation.22 | loop fusion | flops 4194304 | bytes 33558528 | tf_op jit(solution)/shard_map/stack | solution.py:123
  174.4 5.7 %all-to-all-done.1 = bf16[512,2,2,1,128]{4,1,3,2,0:T(2,128)(2,1)S(1)} async-done(((bf16[512,2,2,1,128]{4,1,3,2,0:T(2,128)(2,1)}), bf16[512,2,2,1,128]{4,1,3,2,0:T(2,128)(2,1)S(1)}, u32[]{:S(2)}, u32[]{:S(2)}) %all-to-all-start.1) | async-done | bytes 524320 | tf_op jit(solution)/shard_map/all_to_all | solution.py:105
  180.0 0.3 copy.82
  180.4 0.2 reshape.477
  180.6 6.7 %fusion.26 = f32[16,2,2,2,512]{4,0,3,1,2:T(8,128)S(1)} fusion(bf16[16,2,2,4096,1]{3,0,2,1,4:T(8,128)(2,1)S(1)} %reshape.477, f32[1,4096,512]{2,1,0:T(8,128)} %get-tuple-element.21, f32[1,4096,512]{2,1,0:T(8,128)} %get-tuple-element.20), kind=kOutput, calls=%fused_computation.57 | convolution fusion | flops 545259520 | bytes 17563648 | tf_op jit(solution)/shard_map/...cn,pnw->...pcw/dot_general | solution.py:58
  187.4 6.8 %fusion.13 = f32[16,2,2,2,4096]{4,0,3,1,2:T(8,128)S(1)} fusion(f32[1,512,4096]{2,1,0:T(8,128)} %get-tuple-element.23, f32[1,512,4096]{2,1,0:T(8,128)} %get-tuple-element.22, f32[16,2,2,512]{3,0,1,2:T(8,128)S(1)} %maximum_multiply_fusion.5), kind=kOutput, calls=%fused_computation.25 | convolution fusion | flops 545259520 | bytes 19005440 | tf_op jit(solution)/shard_map/...cn,pnw->...pcw/dot_general | solution.py:58
  194.2 0.1 fusion.65
  194.3 0.1 copy.49
  194.5 0.1 copy.50
  194.6 0.8 pad_maximum_fusion.2
  195.4 5.7 %all-to-all-start.2 = ((bf16[16,2,2,32,128]{4,0,1,2,3:T(8,128)(2,1)}), bf16[16,2,2,32,128]{4,0,1,2,3:T(8,128)(2,1)S(1)}, u32[]{:S(2)}, u32[]{:S(2)}) async-start(bf16[16,2,2,32,128]{4,0,1,2,3:T(8,128)(2,1)} %pad_maximum_fusion.2), calls=%async_computation.2 | async-start | bytes 1048576 | tf_op jit(solution)/shard_map/all_to_all | solution.py:124
  201.1 0.8 gather_fusion
  201.9 0.8 gather_fusion.1
  202.6 0.1 select_bitcast_fusion.5
  202.7 15.1 %all-to-all-done.2 = bf16[16,2,2,32,128]{4,0,1,2,3:T(8,128)(2,1)S(1)} async-done(((bf16[16,2,2,32,128]{4,0,1,2,3:T(8,128)(2,1)}), bf16[16,2,2,32,128]{4,0,1,2,3:T(8,128)(2,1)S(1)}, u32[]{:S(2)}, u32[]{:S(2)}) %all-to-all-start.2) | async-done | bytes 524320 | tf_op jit(solution)/shard_map/all_to_all | solution.py:124
  217.9 0.3 fusion.70
  218.3 0.1 copy.54
  218.4 1.8 broadcast_in_dim.41
  220.2 7.5 %all-to-all-start.3 = ((bf16[8,2,128,2,128]{4,3,2,1,0:T(2,128)(2,1)}), bf16[8,2,128,2,128]{4,3,2,1,0:T(2,128)(2,1)S(1)}, u32[]{:S(2)}, u32[]{:S(2)}) async-start(bf16[8,2,128,2,128]{4,3,2,1,0:T(2,128)(2,1)} %broadcast_in_dim.41), calls=%async_computation.3 | async-start | bytes 2097152 | tf_op jit(solution)/shard_map/all_to_all | solution.py:21
  227.8 0.1 add_select_fusion.5
  227.8 4.5 %fusion.97 = bf16[128,2048]{1,0:T(8,128)(2,1)S(1)} fusion(f32[2048]{0:T(1024)S(1)} %multiply_multiply_fusion, s32[128]{0:T(128)S(1)} %and_select_fusion), kind=kLoop, calls=%fused_computation.153 | loop fusion | flops 5242880 | bytes 532992 | tf_op jit(solution)/shard_map/neg | solution.py:145
  232.4 0.8 copy.55
  233.1 9.0 %all-to-all-done.3 = bf16[8,2,128,2,128]{4,3,2,1,0:T(2,128)(2,1)S(1)} async-done(((bf16[8,2,128,2,128]{4,3,2,1,0:T(2,128)(2,1)}), bf16[8,2,128,2,128]{4,3,2,1,0:T(2,128)(2,1)S(1)}, u32[]{:S(2)}, u32[]{:S(2)}) %all-to-all-start.3) | async-done | bytes 1048608 | tf_op jit(solution)/shard_map/all_to_all | solution.py:21
  242.1 8.1 %fusion.35 = f32[256,256]{0,1:T(8,128)S(1)} fusion(f32[256]{0:T(256)S(1)} %multiply_multiply_fusion.1, s32[256]{0:T(256)S(1)} %iota_add_fusion, s32[2048]{0:T(1024)S(1)} %add_select_fusion.5, bf16[256,8,2,128]{3,2,1,0:T(2,128)(2,1)S(1)} %bitcast.219), kind=kOutput, calls=%fused_computation.66 | convolution fusion | flops 276824064 | bytes 1320960 | tf_op jit(solution)/shard_map/dot_general | solution.py:139
  250.2 8.4 %fusion.38 = f32[256,256]{0,1:T(8,128)S(1)} fusion(f32[256]{0:T(256)S(1)} %multiply_multiply_fusion.1, s32[256]{0:T(256)S(1)} %iota_add_fusion, s32[2048]{0:T(1024)S(1)} %add_select_fusion.5, bf16[256,8,2,128]{3,2,1,0:T(2,128)(2,1)S(1)} %bitcast.220), kind=kOutput, calls=%fused_computation.69 | convolution fusion | flops 277348352 | bytes 1320960 | tf_op jit(solution)/shard_map/dot_general | solution.py:140
  258.7 0.5 convolution_bitcast_fusion.1
  259.2 0.5 convolution_bitcast_fusion
  259.6 1.8 fusion.16
  (40 shorter events, 0.7 us)
Async XLA Ops:
  5.9 2.8 %copy-start = (bf16[128,2048]{1,0:T(8,128)(2,1)}, bf16[128,2048]{1,0:T(8,128)(2,1)S(1)}, u32[]{:S(2)}) copy-start(bf16[128,2048]{1,0:T(8,128)(2,1)S(1)} %get-tuple-element.19) | copy-start | bytes 1572868
  5.9 2.8 %copy-start.2 = (bf16[128,2048]{1,0:T(8,128)(2,1)}, bf16[128,2048]{1,0:T(8,128)(2,1)S(1)}, u32[]{:S(2)}) copy-start(bf16[128,2048]{1,0:T(8,128)(2,1)S(1)} %get-tuple-element.18) | copy-start | bytes 1572868
  5.9 2.3 copy-start.7
  10.0 123.2 %all-to-all-start = ((bf16[8,256,256]{2,1,0:T(8,128)(2,1)}), bf16[8,256,256]{2,1,0:T(8,128)(2,1)}, u32[]{:S(2)}, u32[]{:S(2)}) async-start(bf16[8,256,256]{2,1,0:T(8,128)(2,1)} %broadcast_in_dim.40), calls=%async_computation | async-start | bytes 2097152 | tf_op jit(solution)/shard_map/all_to_all | solution.py:21
  25.3 1.7 copy-start.5
  96.0 17.9 %copy-start.4 = (f32[16,2,512]{2,1,0:T(2,128)S(1)}, f32[16,2,512]{2,1,0:T(2,128)}, u32[]{:S(2)}) copy-start(f32[16,2,512]{2,1,0:T(2,128)} %param.14) | copy-start | bytes 196612
  122.9 9.3 %copy-start.6 = (s32[16]{0:T(128)S(1)}, s32[16]{0:T(128)}, u32[]{:S(2)}) copy-start(s32[16]{0:T(128)} %param.16) | copy-start | bytes 196
  153.8 26.3 %all-to-all-start.1 = ((bf16[512,2,2,1,128]{4,1,3,2,0:T(2,128)(2,1)}), bf16[512,2,2,1,128]{4,1,3,2,0:T(2,128)(2,1)S(1)}, u32[]{:S(2)}, u32[]{:S(2)}) async-start(bf16[512,2,2,1,128]{4,1,3,2,0:T(2,128)(2,1)} %copy.44), calls=%async_computation.1 | async-start | bytes 1048576 | tf_op jit(solution)/shard_map/all_to_all | solution.py:105
  195.4 22.4 %all-to-all-start.2 = ((bf16[16,2,2,32,128]{4,0,1,2,3:T(8,128)(2,1)}), bf16[16,2,2,32,128]{4,0,1,2,3:T(8,128)(2,1)S(1)}, u32[]{:S(2)}, u32[]{:S(2)}) async-start(bf16[16,2,2,32,128]{4,0,1,2,3:T(8,128)(2,1)} %pad_maximum_fusion.2), calls=%async_computation.2 | async-start | bytes 1048576 | tf_op jit(solution)/shard_map/all_to_all | solution.py:124
  220.2 21.9 %all-to-all-start.3 = ((bf16[8,2,128,2,128]{4,3,2,1,0:T(2,128)(2,1)}), bf16[8,2,128,2,128]{4,3,2,1,0:T(2,128)(2,1)S(1)}, u32[]{:S(2)}, u32[]{:S(2)}) async-start(bf16[8,2,128,2,128]{4,3,2,1,0:T(2,128)(2,1)} %broadcast_in_dim.41), calls=%async_computation.3 | async-start | bytes 2097152 | tf_op jit(solution)/shard_map/all_to_all | solution.py:21
  250.2 8.5 %copy-start.1 = (bf16[128,2048]{1,0:T(8,128)(2,1)S(1)}, bf16[128,2048]{1,0:T(8,128)(2,1)}, u32[]{:S(2)}) copy-start(bf16[128,2048]{1,0:T(8,128)(2,1)} %copy-done) | copy-start | bytes 1572868
  250.2 8.5 %copy-start.3 = (bf16[128,2048]{1,0:T(8,128)(2,1)S(1)}, bf16[128,2048]{1,0:T(8,128)(2,1)}, u32[]{:S(2)}) copy-start(bf16[128,2048]{1,0:T(8,128)(2,1)} %copy-done.2) | copy-start | bytes 1572868
where the time goes:
time: 266 us; the launch traced here: 262 us
  local copies, waits for them, and re-layouts  102 us (38%)
  matrix products  52.8 us (20%)
  other arithmetic  44 us (17%)
  starting transfers between devices  30.6 us (12%)
  waiting for transfers between devices  29.7 us (11%)
    gather x2, local copies, waits for them, and re-layouts, shards(): cos_b = jnp.take(cos_full, all_cols, axis=1)  28.1 us
    gather x2, local copies, waits for them, and re-layouts, shards(): sin_b = jnp.take(sin_full, all_cols, axis=1)  26.1 us
    gather x1, local copies, waits for them, and re-layouts, shards(): cos_c = jnp.take(cos_full, all_cols, axis=0)  16.7 us
    gather x1, local copies, waits for them, and re-layouts, shards(): sin_c = jnp.take(sin_full, all_cols, axis=0)  16.7 us
    all_to_all x2, starting transfers between devices, sent_to_all(): lax.all_to_all(jnp.broadcast_to(value[None], (size, *value.shape)), axis,...  15.2 us
    all_to_all x1, waiting for transfers between devices, shards(): lax.all_to_all(as_sent(outgoing.reshape(block_rows, sub_here, 2, count_fa...  15.1 us
    dot_general x2, matrix products, right_apply(): prod = jnp.einsum('...cn,pnw->...pcw', data, table)  13.5 us
    another operation x1, other arithmetic, shards(): jnp.stack([cos_c, -sin_c]) * scale  11.4 us
  transfers between devices with their start and end apart: 4, of which 3 were waited for; matrix products, arithmetic and copies ran while one was open for 51% of the time, Pallas kernels for 0%

commit v1 on v0

v1 whole, which is shorter than its diff:
```python
import functools
import math

import jax
import jax.numpy as jnp
from jax import lax
from jax.experimental import pallas as pl
from jax.experimental.pallas import tpu as pltpu
from jax.sharding import PartitionSpec as P

YF = 2048
M = 128
XM = 512
SUBS = 16
FACETS = 32
TEAM = 8
PAIR = 2
ROWS = 256
BLOCK = 16
MESH = pl.DeviceIdType.MESH
F32 = jnp.float32
BF16 = jnp.bfloat16


def cis(turn, n):
    quarter = n // 4
    q = lax.shift_right_logical(turn + n // 8, quarter.bit_length() - 1)
    x = (turn - q * quarter).astype(F32) * (2.0 * math.pi / n)
    z = x * x
    s = x + x * z * (-1.6666654611e-1 + z * (8.3321608736e-3 - 1.9515295891e-4 * z))
    c = 1.0 - 0.5 * z + z * z * (4.166664568298827e-2 + z * (-1.388731625493765e-3 + 2.443315711809948e-5 * z))
    swap = (q & 1) == 1
    cosine = jnp.where(swap, s, c)
    sine = jnp.where(swap, c, s)
    cosine = jnp.where(((q + 1) & 2) != 0, -cosine, cosine)
    sine = jnp.where((q & 2) != 0, -sine, sine)
    return cosine, sine


def iota(shape, dim):
    return lax.broadcasted_iota(jnp.int32, shape, dim)


def taper(pos):
    _, s = cis(2 * pos + 1, 4 * YF)
    return s * s * (1.0 / math.sqrt(YF))


def dot(a, b):
    return jnp.dot(a, b, preferred_element_type=F32)


def dot_t(a, b):
    return lax.dot_general(a, b, (((0,), (0,)), ((), ())), preferred_element_type=F32)


def round_trip(
    facets, weights, foff, soff, col,
    et_out, q_out, spectra,
    x_buf, hi_c, hi_s, lo_c, lo_s, p_tab, f_tab, r_tab, perm,
    send1, recv1, send2, recv2, send3, recv3, send4, recv4,
    x_sem, s1, r1, s2, r2, s3, r3, s4, r4,
):
    mine = lax.axis_index("facet")
    half = lax.axis_index("half")
    sub = lax.axis_index("sub")
    member = half * 2 + sub

    def mate(i):
        t = lax.rem(member + i, TEAM)
        return t, {"half": t // 2, "sub": lax.rem(t, 2)}

    def peer(i):
        t = lax.rem(mine + i, FACETS)
        return t, {"facet": t}

    load = pltpu.make_async_copy(facets, x_buf, x_sem)
    load.start()

    barrier = pltpu.get_barrier_semaphore()

    @pl.loop(1, TEAM)
    def _(i):
        pl.semaphore_signal(barrier, inc=1, device_id=mate(i)[1], device_id_type=MESH)

    @pl.loop(1, FACETS)
    def _(i):
        pl.semaphore_signal(barrier, inc=1, device_id=peer(i)[1], device_id_type=MESH)

    y = iota((8, YF), 1)
    c, s = cis(((col[0] + 16 * iota((8, YF), 0)) & (YF - 1)) * y & (YF - 1), YF)
    hi_c[...] = c
    hi_s[...] = s
    c, s = cis(iota((16, YF), 0) * iota((16, YF), 1) & (YF - 1), YF)
    w = taper(iota((1, YF), 1))
    lo_c[...] = c * w
    lo_s[...] = s * w

    @pl.loop(0, 8)
    def _(a):
        hc, hs = hi_c[pl.ds(a, 1), :], hi_s[pl.ds(a, 1), :]
        lc, ls = lo_c[...], lo_s[...]
        at = pl.multiple_of(a * 16, 16)
        q_out[pl.ds(at, 16), :] = (hc * lc - hs * ls).astype(BF16)
        q_out[pl.ds(at + M, 16), :] = (-(hs * lc + hc * ls)).astype(BF16)

    turn = foff[mine, 1] & (M - 1)
    k, c = iota((2 * M, 2 * M), 0), iota((2 * M, 2 * M), 1)
    same = ((k & (M - 1)) == ((c - turn) & (M - 1))) & ((k < M) == (c < M))
    perm[...] = jnp.where(same, 1.0, 0.0).astype(BF16)

    first = member * ROWS
    pos = first + iota((16, ROWS), 1)
    c, s = cis(iota((16, ROWS), 0) * pos & (YF - 1), YF)
    w = taper(first + iota((1, ROWS), 1))
    lc, ls = c * w, s * w

    @pl.loop(0, SUBS)
    def _(u):
        freq = (soff[u] + 16 * iota((8, ROWS), 0)) & (YF - 1)
        hc, hs = cis(freq * (first + iota((8, ROWS), 1)) & (YF - 1), YF)
        for a in range(8):
            c, s = hc[a : a + 1], hs[a : a + 1]
            p_tab[u, 16 * a : 16 * a + 16, :] = (c * lc - s * ls).astype(BF16)
            p_tab[u, M + 16 * a : M + 16 * a + 16, :] = (-(s * lc + c * ls)).astype(BF16)

    load.wait()
    q = q_out[...]
    over = (((1,), (1,)), ((), ()))
    from_real = lax.dot_general(x_buf[0], q, over, preferred_element_type=F32)
    from_imag = lax.dot_general(x_buf[1], q, over, preferred_element_type=F32)
    a_both = jnp.concatenate(
        [from_real[:, :M] - from_imag[:, M:], from_real[:, M:] + from_imag[:, :M]], 1
    ).astype(BF16)
    a_both = dot(a_both, perm[...]).astype(BF16)

    pl.semaphore_wait(barrier, TEAM + FACETS - 2)

    def partial(l, t):
        v = dot(p_tab[2 * t + l], a_both)
        return jnp.concatenate([v[:M, :M] - v[M:, M:], v[:M, M:] + v[M:, :M]], 1).astype(BF16)

    for l in range(PAIR):

        @pl.loop(1, TEAM)
        def _(i):
            t, to = mate(i)
            send1[l, i] = partial(l, t)
            pltpu.make_async_remote_copy(
                src_ref=send1.at[l, i], dst_ref=recv1.at[l, i], send_sem=s1.at[l, i], recv_sem=r1.at[l, i],
                device_id=to, device_id_type=MESH,
            ).start()

        recv1[l, 0] = partial(l, member)

    scale = 1.0 / math.sqrt(XM)
    place = (foff[mine, 0] + iota((16, M), 1)) & (XM - 1)
    lc, ls = cis(iota((16, M), 0) * place & (XM - 1), XM)
    lc, ls = lc * scale, ls * scale
    place = (foff[mine, 0] + iota((32, M), 1)) & (XM - 1)
    hc, hs = cis(16 * iota((32, M), 0) * place & (XM - 1), XM)
    for a in range(32):
        c, s = hc[a : a + 1], hs[a : a + 1]
        r_tab[16 * a : 16 * a + 16, :M] = (c * lc - s * ls).astype(BF16)
        r_tab[16 * a : 16 * a + 16, M:] = (s * lc + c * ls).astype(BF16)

    def waited(send, recv, i, l, ssem, rsem):
        return pltpu.make_async_remote_copy(
            src_ref=send.at[l, i], dst_ref=recv.at[l, i], send_sem=ssem.at[l, i], recv_sem=rsem.at[l, i],
            device_id=mate(1)[1], device_id_type=MESH,
        )

    def bulk(send, recv, l, ssem, rsem):
        some = pl.ds(0, FACETS - 1)
        return pltpu.make_async_remote_copy(
            src_ref=send.at[l, some], dst_ref=recv.at[l, some], send_sem=ssem.at[l], recv_sem=rsem.at[l],
            device_id=peer(1)[1], device_id_type=MESH,
        )

    def ship(send, recv, l, i, ssem, rsem):
        t, to = peer(i)
        pltpu.make_async_remote_copy(
            src_ref=send.at[l, t], dst_ref=recv.at[l, mine], send_sem=ssem.at[l], recv_sem=rsem.at[l],
            device_id=to, device_id_type=MESH,
        ).start()

    for l in range(PAIR):
        total = recv1[l, 0].astype(F32)
        for i in range(1, TEAM):
            waited(send1, recv1, i, l, s1, r1).wait_recv()
            total = total + recv1[l, i].astype(F32)
        total = total.astype(BF16)
        cr, ci = total[:, :M], total[:, M:]
        both = jnp.concatenate([jnp.concatenate([cr, ci], 1), jnp.concatenate([ci, -cr], 1)], 0)
        kk = dot(r_tab[...], both).astype(BF16)
        send2[l, :, 0] = kk[:, :M].reshape(FACETS, BLOCK, M)
        send2[l, :, 1] = kk[:, M:].reshape(FACETS, BLOCK, M)

        @pl.loop(1, FACETS)
        def _(i):
            ship(send2, recv2, l, i, s2, r2)

        recv2[l, mine] = send2[l, mine]

    c, s = cis(16 * iota((32, XM), 0) * iota((32, XM), 1) & (XM - 1), XM)
    lc, ls = cis(iota((16, XM), 0) * iota((16, XM), 1) & (XM - 1), XM)
    lc, ls = lc * scale, ls * scale
    for a in range(32):
        hc, hs = c[a : a + 1], s[a : a + 1]
        f_tab[16 * a : 16 * a + 16, :XM] = (hc * lc - hs * ls).astype(BF16)
        f_tab[16 * a : 16 * a + 16, XM:] = (hs * lc + hc * ls).astype(BF16)

    def tiles_of(f):
        o = foff[f, 1]
        lane = iota((BLOCK, M), 1)
        return (lax.shift_right_logical(o, 7) + jnp.where(lane < (o & (M - 1)), 1, 0)) & 3

    for l in range(PAIR):
        bulk(send2, recv2, l, s2, r2).wait_recv()

        def gather(f, acc):
            tile = tiles_of(f)
            got = [recv2[l, f, part].astype(F32) for part in range(2)]
            return tuple(
                acc[4 * part + t] + jnp.where(tile == t, got[part], 0.0) for part in range(2) for t in range(4)
            )

        zero = jnp.zeros((BLOCK, M), F32)
        acc = lax.fori_loop(0, FACETS, gather, (zero,) * 8)
        g = jnp.concatenate([jnp.concatenate(acc[:4], 1), jnp.concatenate(acc[4:], 1)], 0).astype(BF16)
        v = dot(g, f_tab[...])
        weight = weights[:, l, :]
        h_real = weight * (v[:BLOCK, :XM] + v[BLOCK:, XM:])
        h_imag = weight * (v[BLOCK:, :XM] - v[:BLOCK, XM:])
        spectra[:, l, 0, :] = h_real
        spectra[:, l, 1, :] = h_imag
        v = dot(jnp.concatenate([h_real, h_imag], 0).astype(BF16), f_tab[...])
        space = [v[:BLOCK, :XM] - v[BLOCK:, XM:], v[BLOCK:, :XM] + v[:BLOCK, XM:]]

        def window(f):
            tile = tiles_of(f)
            for part in range(2):
                cut = [space[part][:, M * t : M * t + M] for t in range(4)]
                low = jnp.where(tile == 1, cut[1], cut[0])
                high = jnp.where(tile == 3, cut[3], cut[2])
                send3[l, f, part] = jnp.where(tile < 2, low, high).astype(BF16)

        @pl.loop(1, FACETS)
        def _(i):
            window(peer(i)[0])
            ship(send3, recv3, l, i, s3, r3)

        window(mine)
        recv3[l, mine] = send3[l, mine]

    for l in range(PAIR):
        bulk(send3, recv3, l, s3, r3).wait_recv()
        rows = jnp.concatenate([recv3[l, :, 0].reshape(XM, M), recv3[l, :, 1].reshape(XM, M)], 1)
        u = dot_t(rows, r_tab[...])
        send4[l] = jnp.concatenate([u[:M, :M] - u[M:, M:], u[M:, :M] + u[:M, M:]], 1).astype(BF16)

        @pl.loop(1, TEAM)
        def _(i):
            pltpu.make_async_remote_copy(
                src_ref=send4.at[l], dst_ref=recv4.at[l, i], send_sem=s4.at[l, i], recv_sem=r4.at[l, i],
                device_id=mate(i)[1], device_id_type=MESH,
            ).start()

        recv4[l, 0] = send4[l]

    def spread(l, i):
        d = recv4[l, i]
        d = jnp.concatenate([d, jnp.concatenate([d[:, M:], -d[:, :M]], 1)], 0)
        t = lax.rem(member - i + TEAM, TEAM)
        return dot(d, p_tab[2 * t + l])

    e = spread(0, 0) + spread(1, 0)
    for l in range(PAIR):
        for i in range(1, TEAM):
            pltpu.make_async_remote_copy(
                src_ref=send4.at[l], dst_ref=recv4.at[l, i], send_sem=s4.at[l, i], recv_sem=r4.at[l, i],
                device_id=mate(1)[1], device_id_type=MESH,
            ).wait_recv()
            e = e + spread(l, i)
    et_out[...] = dot(perm[...], e.astype(BF16)).astype(BF16)

    for l in range(PAIR):
        bulk(send2, recv2, l, s2, r2).wait_send()
        bulk(send3, recv3, l, s3, r3).wait_send()
        for i in range(1, TEAM):
            waited(send1, recv1, i, l, s1, r1).wait_send()
            pltpu.make_async_remote_copy(
                src_ref=send4.at[l], dst_ref=recv4.at[l, i], send_sem=s4.at[l, i], recv_sem=r4.at[l, i],
                device_id=mate(1)[1], device_id_type=MESH,
            ).wait_send()


def correction(et, q, out):
    gain = 2.0 * math.sqrt(YF / M)
    e = et[...]
    out[0, 0] = (dot_t(e, q[...]) * gain).astype(BF16)
    out[0, 1] = (dot_t(jnp.concatenate([e[M:], -e[:M]], 0), q[...]) * gain).astype(BF16)


def shards(facets, weights, facet_offsets, subgrid_offsets, column):
    smem = pl.BlockSpec(memory_space=pltpu.SMEM)
    vmem = pl.BlockSpec(memory_space=pltpu.VMEM)
    dma = pltpu.SemaphoreType.DMA
    et, q, spectra = pl.pallas_call(
        round_trip,
        out_shape=(
            jax.ShapeDtypeStruct((2 * M, ROWS), BF16),
            jax.ShapeDtypeStruct((2 * M, YF), BF16),
            jax.ShapeDtypeStruct((BLOCK, PAIR, 2, XM), F32),
        ),
        in_specs=[pl.BlockSpec(memory_space=pl.ANY), vmem, smem, smem, smem],
        out_specs=(vmem, vmem, vmem),
        scratch_shapes=[
            pltpu.VMEM((2, ROWS, YF), BF16),
            pltpu.VMEM((8, YF), F32),
            pltpu.VMEM((8, YF), F32),
            pltpu.VMEM((16, YF), F32),
            pltpu.VMEM((16, YF), F32),
            pltpu.VMEM((SUBS, 2 * M, ROWS), BF16),
            pltpu.VMEM((XM, 2 * XM), BF16),
            pltpu.VMEM((XM, 2 * M), BF16),
            pltpu.VMEM((2 * M, 2 * M), BF16),
            pltpu.VMEM((PAIR, TEAM, M, 2 * M), BF16),
            pltpu.VMEM((PAIR, TEAM, M, 2 * M), BF16),
            pltpu.VMEM((PAIR, FACETS, 2, BLOCK, M), BF16),
            pltpu.VMEM((PAIR, FACETS, 2, BLOCK, M), BF16),
            pltpu.VMEM((PAIR, FACETS, 2, BLOCK, M), BF16),
            pltpu.VMEM((PAIR, FACETS, 2, BLOCK, M), BF16),
            pltpu.VMEM((PAIR, M, 2 * M), BF16),
            pltpu.VMEM((PAIR, TEAM, M, 2 * M), BF16),
            dma,
            dma((PAIR, TEAM)), dma((PAIR, TEAM)),
            dma((PAIR,)), dma((PAIR,)),
            dma((PAIR,)), dma((PAIR,)),
            dma((PAIR, TEAM)), dma((PAIR, TEAM)),
        ],
        compiler_params=pltpu.CompilerParams(
            collective_id=0, has_side_effects=True, vmem_limit_bytes=40 * 2**20
        ),
        cost_estimate=pl.CostEstimate(flops=3 * 10**9, bytes_accessed=4 * 10**6, transcendentals=0),
        name="round_trip",
    )(facets[0], weights, facet_offsets, subgrid_offsets, column)
    part = 512
    update = pl.pallas_call(
        correction,
        grid=(YF // part,),
        out_shape=jax.ShapeDtypeStruct((1, 2, ROWS, YF), BF16),
        in_specs=[
            pl.BlockSpec((2 * M, ROWS), lambda i: (0, 0)),
            pl.BlockSpec((2 * M, part), lambda i: (0, i)),
        ],
        out_specs=pl.BlockSpec((1, 2, ROWS, part), lambda i: (0, 0, 0, i)),
        name="correction",
    )(et, q)
    return update, spectra


def solution(mesh):
    return jax.shard_map(
        shards,
        mesh=mesh,
        in_specs=(
            P("facet", None, ("half", "sub"), None),
            P("facet", ("half", "sub"), None),
            P(),
            P(),
            P(),
        ),
        out_specs=(
            P("facet", None, ("half", "sub"), None),
            P("facet", ("half", "sub"), None, None),
        ),
        check_vma=False,
    )
```

time: 266 us -> 72.9 us (0.27); the launches traced: 262 us -> 71.9 us
  local copies, waits for them, and re-layouts: 102 us -> 6.12 us
  Pallas kernels: 0 us -> 64.5 us
  matrix products: 52.8 us -> 0 us
  other arithmetic: 44 us -> 0 us
  starting transfers between devices: 30.6 us -> 0 us
  waiting for transfers between devices: 29.7 us -> 0 us
    gather x12 -> x0, local copies, waits for them, and re-layouts: 93.9 us -> none  [the longest x2 28.1 us: shards(): cos_b = jnp.take(cos_full, all_cols, axis=1)]
    pallas_call x0 -> x2, Pallas kernels: none -> 64.5 us  [the longest x1 60.3 us: shards(): pl.pallas_call(round_trip, out_shape=(jax.ShapeDtypeStruct((2 * M, ROWS),...]
    dot_general x12 -> x0, matrix products: 52.8 us -> none  [the longest x2 13.5 us: right_apply(): prod = jnp.einsum('...cn,pnw->...pcw', data, table)]
    all_to_all x4 -> x0, starting transfers between devices: 30.6 us -> none  [the longest x2 15.2 us: sent_to_all(): lax.all_to_all(jnp.broadcast_to(value[None], (size, *value.shape)), axis,...]
    all_to_all x4 -> x0, waiting for transfers between devices: 29.7 us -> none  [the longest x1 15.1 us: shards(): lax.all_to_all(as_sent(outgoing.reshape(block_rows, sub_here, 2, count_fa...]
    another operation x12 -> x0, other arithmetic: 23.6 us -> none  [the longest x1 11.4 us: shards(): jnp.stack([cos_c, -sin_c]) * scale]
    convert_element_type x3 -> x0, other arithmetic: 6.4 us -> none  [the longest x1 4.57 us: facet_table(): (-sine * shaped).astype(jnp.bfloat16)]
    unnamed x20 -> x12, local copies, waits for them, and re-layouts: 1.05 us -> 6.12 us
  transfers between devices with their start and end apart: 4 -> 0, of which waited for: 3 -> 0; matrix products, arithmetic and copies ran while one was open for 51% -> 0% of each run, Pallas kernels for 0% -> 0%
where the time goes in v1:
time: 72.9 us; the launch traced here: 71.9 us
  Pallas kernels  64.5 us (88%)
  local copies, waits for them, and re-layouts  6.12 us (8%)
  between operations  1.3 us (2%)
    pallas_call x1, Pallas kernels, shards(): pl.pallas_call(round_trip, out_shape=(jax.ShapeDtypeStruct((2 * M, ROWS),...  60.3 us
    unnamed x12, local copies, waits for them, and re-layouts  6.12 us
    pallas_call x1, Pallas kernels, shards(): pl.pallas_call(correction, grid=(YF // part,), out_shape=jax.ShapeDtypeSt...  4.19 us

profile of v1, /device:TPU:1, one launch (start us, length us, event | category | flops | bytes accessed | tf_op | source)
XLA Modules:
  0.0 71.9 jit_solution(13269403295843682914)
XLA Ops:
  1.3 0.8 %copy.7.foff = s32[32,2]{1,0:T(8,128)S(1)} copy(s32[32,2]{0,1:T(2,128)} %param.7) | data formatting | bytes 512 | tf_op args[2]
  2.0 0.0 copy-start.2
  2.0 1.6 %copy-done.2 = bf16[1,2,256,2048]{3,2,1,0:T(8,128)(2,1)S(1)} copy-done((bf16[1,2,256,2048]{3,2,1,0:T(8,128)(2,1)S(1)}, bf16[1,2,256,2048]{3,2,1,0:T(8,128)(2,1)}, u32[]{:S(2)}) %copy-start.2) | copy-done | bytes 2097176
  3.6 0.0 copy-start.3
  3.6 0.8 %copy-done.3 = f32[16,2,512]{2,1,0:T(2,128)S(1)} copy-done((f32[16,2,512]{2,1,0:T(2,128)S(1)}, f32[16,2,512]{2,1,0:T(2,128)}, u32[]{:S(2)}) %copy-start.3) | copy-done | bytes 65560
  4.5 0.0 copy-start.4
  4.5 0.7 copy-done.4
  5.1 60.3 %round_trip.1 = (bf16[256,256]{1,0:T(8,128)(2,1)S(1)}, bf16[256,2048]{1,0:T(8,128)(2,1)S(1)}, f32[16,2,2,512]{3,2,1,0:T(2,128)S(1)}) custom-call(bf16[2,256,2048]{2,1,0:T(8,128)(2,1)S(1)} %bitcast.1, f32[16,2,512]{2,1,0:T(2,128)S(1)} %copy-done.3, s32[32,2]{1,0:T(8,128)S(1)} %copy.7.foff, s32[16]{0:T(128)S(1)} %copy-done.4, s32[1]{0:T(128)S(6)} %copy.9.col), custom_call_target="tpu_custom_call" | custom-call | flops 3000000000 | bytes 4000000 | tf_op jit(solution)/shard_map/round_trip/pallas_call | solution.py:309
  65.4 0.0 copy-start
  65.4 1.0 %copy-done = bf16[256,2048]{1,0:T(8,128)(2,1)} copy-done((bf16[256,2048]{1,0:T(8,128)(2,1)}, bf16[256,2048]{1,0:T(8,128)(2,1)S(1)}, u32[]{:S(2)}) %copy-start) | copy-done | bytes 1048600
  66.4 0.0 copy-start.1
  66.4 0.7 copy-done.1
  67.1 4.2 %correction.1 = bf16[1,2,256,2048]{3,2,1,0:T(8,128)(2,1)} custom-call(bf16[256,256]{1,0:T(8,128)(2,1)} %copy-done.1, bf16[256,2048]{1,0:T(8,128)(2,1)} %copy-done), custom_call_target="tpu_custom_call" | custom-call | tf_op jit(solution)/shard_map/correction/pallas_call | solution.py:349
  71.3 0.7 copy.10
Async XLA Ops:
  2.0 1.6 %copy-start.2 = (bf16[1,2,256,2048]{3,2,1,0:T(8,128)(2,1)S(1)}, bf16[1,2,256,2048]{3,2,1,0:T(8,128)(2,1)}, u32[]{:S(2)}) copy-start(bf16[1,2,256,2048]{3,2,1,0:T(8,128)(2,1)} %param.5) | copy-start | bytes 6291460
  3.6 0.8 %copy-start.3 = (f32[16,2,512]{2,1,0:T(2,128)S(1)}, f32[16,2,512]{2,1,0:T(2,128)}, u32[]{:S(2)}) copy-start(f32[16,2,512]{2,1,0:T(2,128)} %weights.1) | copy-start | bytes 196612
  4.5 0.7 copy-start.4
  65.4 1.0 %copy-start = (bf16[256,2048]{1,0:T(8,128)(2,1)}, bf16[256,2048]{1,0:T(8,128)(2,1)S(1)}, u32[]{:S(2)}) copy-start(bf16[256,2048]{1,0:T(8,128)(2,1)S(1)} %get-tuple-element.6.q) | copy-start | bytes 3145732
  66.4 0.7 copy-start.1

commit v2 on v1

v2 whole, which is shorter than its diff:
```python
import functools
import math

import jax
import jax.numpy as jnp
from jax import lax
from jax.experimental import pallas as pl
from jax.experimental.pallas import tpu as pltpu
from jax.sharding import PartitionSpec as P

YF = 2048
M = 128
XM = 512
SUBS = 16
FACETS = 32
PAIR = 2
ROWS = 256
BLOCK = 16
VMEM_MIB = 60
MESH = pl.DeviceIdType.MESH
F32 = jnp.float32
BF16 = jnp.bfloat16


def cis(turn, n):
    quarter = n // 4
    q = lax.shift_right_logical(turn + n // 8, quarter.bit_length() - 1)
    x = (turn - q * quarter).astype(F32) * (2.0 * math.pi / n)
    z = x * x
    s = x + x * z * (-1.6666654611e-1 + z * (8.3321608736e-3 - 1.9515295891e-4 * z))
    c = 1.0 - 0.5 * z + z * z * (4.166664568298827e-2 + z * (-1.388731625493765e-3 + 2.443315711809948e-5 * z))
    swap = (q & 1) == 1
    cosine = jnp.where(swap, s, c)
    sine = jnp.where(swap, c, s)
    cosine = jnp.where(((q + 1) & 2) != 0, -cosine, cosine)
    sine = jnp.where((q & 2) != 0, -sine, sine)
    return cosine, sine


def iota(shape, dim):
    return lax.broadcasted_iota(jnp.int32, shape, dim)


def taper(pos):
    _, s = cis(2 * pos + 1, 4 * YF)
    return s * s * (1.0 / math.sqrt(YF))


def dot(a, b):
    return jnp.dot(a, b, preferred_element_type=F32)


def dot_t(a, b):
    return lax.dot_general(a, b, (((0,), (0,)), ((), ())), preferred_element_type=F32)


def remote(src, dst, send, recv, to):
    return pltpu.make_async_remote_copy(
        src_ref=src, dst_ref=dst, send_sem=send, recv_sem=recv, device_id=to, device_id_type=MESH
    )


def round_trip(
    facets, weights, foff_in, soff_in, col_in,
    et_out, q_out, spectra,
    foff, soff, col, x_buf, w_buf, hi_c, hi_s, lo_c, lo_s, p_tab, f_tab, r_tab, perm,
    a_buf, send1, recv1, send2, mid2, recv2, recv3, win3, rows3, recv4, send5, recv5,
    small_sem, x_sem, w_sem, sa, ra, s1, r1, s2, r2, sz2, rz2, sz3, rz3, s3, r3, s4, r4, s5, r5,
):
    mine = lax.axis_index("facet")
    x = lax.axis_index("half")
    hi = lax.axis_index("sub")
    core = lax.rem(mine, 2)
    z = lax.rem(mine // 2, 8)
    low = mine // 16
    slot = low * 2 + core

    def at_x(d):
        return {"half": lax.rem(x + d, 4)}

    def at_z(d):
        return {"facet": low * 16 + lax.rem(z + d, 8) * 2 + core}

    def slot_of(q):
        return lax.rem(low + q // 2, 2) * 2 + lax.rem(core + q % 2, 2)

    def at_slot(q):
        return {"facet": lax.rem(low + q // 2, 2) * 16 + z * 2 + lax.rem(core + q % 2, 2)}

    across = {"sub": 1 - hi}

    smalls = [
        pltpu.make_async_copy(src, dst, small_sem.at[i])
        for i, (src, dst) in enumerate([(col_in, col), (foff_in, foff), (soff_in, soff)])
    ]
    for copy in smalls:
        copy.start()
    load = pltpu.make_async_copy(facets.at[0], x_buf, x_sem)
    load.start()
    load_w = pltpu.make_async_copy(weights, w_buf, w_sem)
    load_w.start()

    barrier = pltpu.get_barrier_semaphore()
    friends = [across] + [at_x(d) for d in (1, 2, 3)] + [at_slot(q) for q in (1, 2, 3)] + [at_z(d) for d in range(1, 8)]
    for to in friends:
        pl.semaphore_signal(barrier, inc=1, device_id=to, device_id_type=MESH)

    y = iota((8, YF), 1)
    c, s = cis(iota((16, YF), 0) * iota((16, YF), 1) & (YF - 1), YF)
    w = taper(iota((1, YF), 1))
    lo_c[...] = c * w
    lo_s[...] = s * w
    for copy in smalls:
        copy.wait()
    c, s = cis(((col[0] + 16 * iota((8, YF), 0)) & (YF - 1)) * y & (YF - 1), YF)
    hi_c[...] = c
    hi_s[...] = s

    @pl.loop(0, 8)
    def _(a):
        hc, hs = hi_c[pl.ds(a, 1), :], hi_s[pl.ds(a, 1), :]
        lc, ls = lo_c[...], lo_s[...]
        at = pl.multiple_of(a * 16, 16)
        q_out[pl.ds(at, 16), :] = (hc * lc - hs * ls).astype(BF16)
        q_out[pl.ds(at + M, 16), :] = (-(hs * lc + hc * ls)).astype(BF16)

    turn = foff[1, mine] & (M - 1)
    k, c = iota((2 * M, 2 * M), 0), iota((2 * M, 2 * M), 1)
    same = ((k & (M - 1)) == ((c - turn) & (M - 1))) & ((k < M) == (c < M))
    perm[...] = jnp.where(same, 1.0, 0.0).astype(BF16)

    load.wait()
    q = q_out[...]
    over = (((1,), (1,)), ((), ()))
    from_real = lax.dot_general(x_buf[0], q, over, preferred_element_type=F32)
    from_imag = lax.dot_general(x_buf[1], q, over, preferred_element_type=F32)
    a_both = jnp.concatenate(
        [from_real[:, :M] - from_imag[:, M:], from_real[:, M:] + from_imag[:, :M]], 1
    ).astype(BF16)
    a_buf[hi] = dot(a_both, perm[...]).astype(BF16)

    pl.semaphore_wait(barrier, len(friends))
    swap_a = remote(a_buf.at[hi], a_buf.at[hi], sa, ra, across)
    swap_a.start()

    first = x * (2 * ROWS)
    pos = first + iota((16, 2 * ROWS), 1)
    c, s = cis(iota((16, 2 * ROWS), 0) * pos & (YF - 1), YF)
    w = taper(first + iota((1, 2 * ROWS), 1))
    lc, ls = c * w, s * w

    @pl.loop(0, 2 * 4)
    def _(u):
        freq = (soff[4 * (u // 2) + 2 * hi + lax.rem(u, 2)] + 16 * iota((8, 2 * ROWS), 0)) & (YF - 1)
        hc, hs = cis(freq * (first + iota((8, 2 * ROWS), 1)) & (YF - 1), YF)
        for a in range(8):
            c, s = hc[a : a + 1], hs[a : a + 1]
            real = (c * lc - s * ls).astype(BF16)
            imag = (-(s * lc + c * ls)).astype(BF16)
            for b in range(2):
                p_tab[b, u, 16 * a : 16 * a + 16, :] = real[:, ROWS * b : ROWS * b + ROWS]
                p_tab[b, u, M + 16 * a : M + 16 * a + 16, :] = imag[:, ROWS * b : ROWS * b + ROWS]

    def partial(l, to_x):
        u = 2 * to_x + l
        v = dot(p_tab[0, u], a_buf[0]) + dot(p_tab[1, u], a_buf[1])
        return jnp.concatenate([v[:M, :M] - v[M:, M:], v[:M, M:] + v[M:, :M]], 1).astype(BF16)

    swap_a.wait()
    for l in range(PAIR):
        for d in (2, 1, 3):
            send1[l, d] = partial(l, lax.rem(x + d, 4))
            remote(send1.at[l, d], recv1.at[l, d], s1.at[l, d], r1.at[l, d], at_x(d)).start()
        recv1[l, 0] = partial(l, x)

    scale = 1.0 / math.sqrt(XM)
    place = (foff[0, mine] + iota((16, M), 1)) & (XM - 1)
    lc, ls = cis(iota((16, M), 0) * place & (XM - 1), XM)
    lc, ls = lc * scale, ls * scale
    place = (foff[0, mine] + iota((32, M), 1)) & (XM - 1)
    i = iota((32, M), 0)
    block = (i & 16) + 2 * (i & 7) + (lax.shift_right_logical(i, 3) & 1)
    hc, hs = cis(16 * block * place & (XM - 1), XM)
    for a in range(32):
        c, s = hc[a : a + 1], hs[a : a + 1]
        r_tab[16 * a : 16 * a + 16, :M] = (c * lc - s * ls).astype(BF16)
        r_tab[16 * a : 16 * a + 16, M:] = (s * lc + c * ls).astype(BF16)

    c, s = cis(16 * iota((32, XM), 0) * iota((32, XM), 1) & (XM - 1), XM)
    lc, ls = cis(iota((16, XM), 0) * iota((16, XM), 1) & (XM - 1), XM)
    lc, ls = lc * scale, ls * scale
    for a in range(32):
        hc, hs = c[a : a + 1], s[a : a + 1]
        f_tab[16 * a : 16 * a + 16, :XM] = (hc * lc - hs * ls).astype(BF16)
        f_tab[16 * a : 16 * a + 16, XM:] = (hs * lc + hc * ls).astype(BF16)

    far = (4, 3, 5, 2, 6, 1, 7)
    near = (1, 7, 2, 6, 3, 5, 4)

    for l in range(PAIR):
        total = recv1[l, 0].astype(F32)
        for d in (1, 3, 2):
            remote(send1.at[l, d], recv1.at[l, d], s1.at[l, d], r1.at[l, d], at_x(d)).wait_recv()
            total = total + recv1[l, d].astype(F32)
        total = total.astype(BF16)
        cr, ci = total[:, :M], total[:, M:]
        both = jnp.concatenate([jnp.concatenate([cr, ci], 1), jnp.concatenate([ci, -cr], 1)], 0)
        kk = dot(r_tab[...], both).astype(BF16)
        send2[l, :, :, 0] = kk[:, :M].reshape(4, 8, BLOCK, M)
        send2[l, :, :, 1] = kk[:, M:].reshape(4, 8, BLOCK, M)
        for q in (3, 2, 1):
            remote(send2.at[l, slot_of(q)], mid2.at[l, slot], s2.at[l, q], r2.at[l, q], at_slot(q)).start()
        mid2[l, slot] = send2[l, slot]

    def z2(l, d):
        return remote(
            mid2.at[l, :, lax.rem(z + d, 8)], recv2.at[l, z], sz2.at[l, d], rz2.at[l, d], at_z(d)
        )

    for l in range(PAIR):
        for q in (1, 2, 3):
            remote(send2.at[l, slot_of(q)], mid2.at[l, slot_of(q)], s2.at[l, q], r2.at[l, q], at_slot(q)).wait_recv()
        for d in far:
            z2(l, d).start()

    lane = iota((BLOCK, M), 1)

    def tiles_of(f):
        o = foff[1, f]
        return (lax.shift_right_logical(o, 7) + jnp.where(lane < (o & (M - 1)), 1, 0)) & 3

    load_w.wait()
    for l in range(PAIR):
        acc = [[jnp.zeros((BLOCK, M), F32) for _ in range(4)] for _ in range(2)]
        for d in (0,) + near:
            from_z = lax.rem(z + 8 - d, 8)
            if d:
                remote(recv2.at[l, from_z], recv2.at[l, from_z], sz2.at[l, d], rz2.at[l, d], at_z(d)).wait_recv()
            for q in range(4):
                tile = tiles_of((q // 2) * 16 + from_z * 2 + q % 2)
                for part in range(2):
                    got = (recv2[l, from_z, q, part] if d else mid2[l, q, z, part]).astype(F32)
                    for t in range(4):
                        acc[part][t] = acc[part][t] + jnp.where(tile == t, got, 0.0)
        g = jnp.concatenate([jnp.concatenate(acc[0], 1), jnp.concatenate(acc[1], 1)], 0).astype(BF16)
        v = dot(g, f_tab[...])
        weight = w_buf[:, l, :]
        h_real = weight * (v[:BLOCK, :XM] + v[BLOCK:, XM:])
        h_imag = weight * (v[BLOCK:, :XM] - v[:BLOCK, XM:])
        v = dot(jnp.concatenate([h_real, h_imag], 0).astype(BF16), f_tab[...])
        recv3[l, z, 0] = (v[:BLOCK, :XM] - v[BLOCK:, XM:]).astype(BF16)
        recv3[l, z, 1] = (v[BLOCK:, :XM] + v[:BLOCK, XM:]).astype(BF16)
        for d in far:
            remote(recv3.at[l, z], recv3.at[l, z], sz3.at[l, d], rz3.at[l, d], at_z(d)).start()
        spectra[:, l, 0, :] = h_real
        spectra[:, l, 1, :] = h_imag

    for l in range(PAIR):
        tiles = [tiles_of(lax.rem(low + q // 2, 2) * 16 + z * 2 + lax.rem(core + q % 2, 2)) for q in range(4)]
        for d in (0,) + near:
            from_z = lax.rem(z + 8 - d, 8)
            if d:
                remote(recv3.at[l, from_z], recv3.at[l, from_z], sz3.at[l, d], rz3.at[l, d], at_z(d)).wait_recv()
            for part in range(2):
                whole = recv3[l, from_z, part].astype(F32)
                cut = [whole[:, M * t : M * t + M] for t in range(4)]
                for q in range(4):
                    one = jnp.where(tiles[q] == 1, cut[1], cut[0])
                    two = jnp.where(tiles[q] == 3, cut[3], cut[2])
                    one = jnp.where(tiles[q] < 2, one, two).astype(BF16)
                    if q:
                        win3[l, q, from_z, part] = one
                    else:
                        rows3[l, slot, from_z, part] = one
        for q in (3, 2, 1):
            remote(win3.at[l, q], rows3.at[l, slot], s3.at[l, q], r3.at[l, q], at_slot(q)).start()

    e_here = e_there = None
    for l in range(PAIR):
        for q in (1, 2, 3):
            remote(win3.at[l, q], rows3.at[l, slot_of(q)], s3.at[l, q], r3.at[l, q], at_slot(q)).wait_recv()
        rows = jnp.concatenate([rows3[l, :, :, 0].reshape(XM, M), rows3[l, :, :, 1].reshape(XM, M)], 1)
        u = dot_t(rows, r_tab[...])
        recv4[l, x] = jnp.concatenate([u[:M, :M] - u[M:, M:], u[M:, :M] + u[:M, M:]], 1).astype(BF16)
        for d in (2, 1, 3):
            remote(recv4.at[l, x], recv4.at[l, x], s4.at[l, d], r4.at[l, d], at_x(d)).start()

    for l in range(PAIR):
        for d in (0, 1, 3, 2):
            from_x = lax.rem(x + 4 - d, 4)
            if d:
                remote(recv4.at[l, from_x], recv4.at[l, from_x], s4.at[l, d], r4.at[l, d], at_x(d)).wait_recv()
            v = recv4[l, from_x]
            v = jnp.concatenate([v, jnp.concatenate([v[:, M:], -v[:, :M]], 1)], 0)
            there = dot(v, p_tab[1 - hi, 2 * from_x + l])
            here = dot(v, p_tab[hi, 2 * from_x + l])
            e_there = there if e_there is None else e_there + there
            e_here = here if e_here is None else e_here + here
    send5[...] = e_there.astype(BF16)
    swap_e = remote(send5, recv5, s5, r5, across)
    swap_e.start()
    swap_e.wait_recv()
    e = (e_here + recv5[...].astype(F32)).astype(BF16)
    et_out[...] = dot(perm[...], e).astype(BF16)

    swap_e.wait_send()
    for l in range(PAIR):
        for d in range(1, 4):
            remote(send1.at[l, d], recv1.at[l, d], s1.at[l, d], r1.at[l, d], at_x(d)).wait_send()
            remote(recv4.at[l, x], recv4.at[l, x], s4.at[l, d], r4.at[l, d], at_x(d)).wait_send()
            remote(send2.at[l, slot_of(d)], mid2.at[l, slot], s2.at[l, d], r2.at[l, d], at_slot(d)).wait_send()
            remote(win3.at[l, d], rows3.at[l, slot], s3.at[l, d], r3.at[l, d], at_slot(d)).wait_send()
        for d in range(1, 8):
            z2(l, d).wait_send()
            remote(recv3.at[l, z], recv3.at[l, z], sz3.at[l, d], rz3.at[l, d], at_z(d)).wait_send()


def correction(et, q, spectra_in, out, spectra, buf, sems, sem):
    copy = pltpu.make_async_copy(spectra_in, spectra, sem)
    copy.start()
    gain = 2.0 * math.sqrt(YF / M)
    real = et[...]
    imag = jnp.concatenate([real[M:], -real[:M]], 0)
    parts = buf.shape[0]
    width = buf.shape[3]
    moves = []
    for i in range(parts):
        table = q[:, width * i : width * i + width]
        buf[i, 0] = (dot_t(real, table) * gain).astype(BF16)
        buf[i, 1] = (dot_t(imag, table) * gain).astype(BF16)
        move = pltpu.make_async_copy(buf.at[i], out.at[0, :, :, pl.ds(width * i, width)], sems.at[i])
        move.start()
        moves.append(move)
    for move in moves:
        move.wait()
    copy.wait()


def shards(facets, weights, facet_offsets, subgrid_offsets, column):
    hbm = pl.BlockSpec(memory_space=pl.ANY)
    vmem = pl.BlockSpec(memory_space=pltpu.VMEM)
    dma = pltpu.SemaphoreType.DMA
    pair_of = lambda *shape: pltpu.VMEM((PAIR, *shape), BF16)
    et, q, spectra = pl.pallas_call(
        round_trip,
        out_shape=(
            jax.ShapeDtypeStruct((2 * M, ROWS), BF16),
            jax.ShapeDtypeStruct((2 * M, YF), BF16),
            jax.ShapeDtypeStruct((BLOCK, PAIR, 2, XM), F32),
        ),
        in_specs=[hbm] * 5,
        out_specs=(vmem, vmem, vmem),
        scratch_shapes=[
            pltpu.SMEM((2, FACETS), jnp.int32),
            pltpu.SMEM((SUBS,), jnp.int32),
            pltpu.SMEM((1,), jnp.int32),
            pltpu.VMEM((2, ROWS, YF), BF16),
            pltpu.VMEM((BLOCK, PAIR, XM), F32),
            pltpu.VMEM((8, YF), F32),
            pltpu.VMEM((8, YF), F32),
            pltpu.VMEM((16, YF), F32),
            pltpu.VMEM((16, YF), F32),
            pltpu.VMEM((2, 8, 2 * M, ROWS), BF16),
            pltpu.VMEM((XM, 2 * XM), BF16),
            pltpu.VMEM((XM, 2 * M), BF16),
            pltpu.VMEM((2 * M, 2 * M), BF16),
            pltpu.VMEM((2, ROWS, 2 * M), BF16),
            pair_of(4, M, 2 * M),
            pair_of(4, M, 2 * M),
            pair_of(4, 8, 2, BLOCK, M),
            pair_of(4, 8, 2, BLOCK, M),
            pair_of(8, 4, 2, BLOCK, M),
            pair_of(8, 2, BLOCK, XM),
            pair_of(4, 8, 2, BLOCK, M),
            pair_of(4, 8, 2, BLOCK, M),
            pair_of(4, M, 2 * M),
            pltpu.VMEM((2 * M, ROWS), BF16),
            pltpu.VMEM((2 * M, ROWS), BF16),
            dma((3,)), dma, dma,
            dma, dma,
            dma((PAIR, 4)), dma((PAIR, 4)),
            dma((PAIR, 4)), dma((PAIR, 4)),
            dma((PAIR, 8)), dma((PAIR, 8)),
            dma((PAIR, 8)), dma((PAIR, 8)),
            dma((PAIR, 4)), dma((PAIR, 4)),
            dma((PAIR, 4)), dma((PAIR, 4)),
            dma, dma,
        ],
        compiler_params=pltpu.CompilerParams(
            collective_id=0, has_side_effects=True, vmem_limit_bytes=VMEM_MIB * 2**20
        ),
        cost_estimate=pl.CostEstimate(flops=3 * 10**9, bytes_accessed=4 * 10**6, transcendentals=0),
        name="round_trip",
    )(facets, weights, facet_offsets.T, subgrid_offsets, column)
    parts = 4
    update, spectra = pl.pallas_call(
        correction,
        out_shape=(
            jax.ShapeDtypeStruct((1, 2, ROWS, YF), BF16),
            jax.ShapeDtypeStruct((BLOCK, PAIR, 2, XM), F32),
        ),
        in_specs=[vmem, vmem, hbm],
        out_specs=(hbm, hbm),
        scratch_shapes=[
            pltpu.VMEM((parts, 2, ROWS, YF // parts), BF16),
            dma((parts,)),
            dma,
        ],
        compiler_params=pltpu.CompilerParams(vmem_limit_bytes=24 * 2**20),
        cost_estimate=pl.CostEstimate(flops=10**9, bytes_accessed=3 * 10**6, transcendentals=0),
        name="correction",
    )(et, q, spectra)
    return update, spectra


def solution(mesh):
    return jax.shard_map(
        shards,
        mesh=mesh,
        in_specs=(
            P("facet", None, ("half", "sub"), None),
            P("facet", ("half", "sub"), None),
            P(),
            P(),
            P(),
        ),
        out_specs=(
            P("facet", None, ("half", "sub"), None),
            P("facet", ("half", "sub"), None, None),
        ),
        check_vma=False,
    )
```

time: 72.9 us -> 70.7 us (0.970)
  the two profiles are of different devices: /device:TPU:1 before, /device:TPU:2 now
where the time goes in v2:
time: 70.7 us; the launch traced here: 70.5 us
  Pallas kernels  66.2 us (94%)
  local copies, waits for them, and re-layouts  3.03 us (4%)
  between operations  1.3 us (2%)
    pallas_call x1, Pallas kernels, shards(): pl.pallas_call(round_trip, out_shape=(jax.ShapeDtypeStruct((2 * M, ROWS),...  64.5 us
    unnamed x6, local copies, waits for them, and re-layouts  3.03 us
    pallas_call x1, Pallas kernels, shards(): pl.pallas_call(correction, out_shape=(jax.ShapeDtypeStruct((1, 2, ROWS, Y...  1.68 us

profile of v2, /device:TPU:2, one launch (start us, length us, event | category | flops | bytes accessed | tf_op | source)
XLA Modules:
  0.0 70.5 jit_solution(3818595023712428105)
XLA Ops:
  1.3 64.5 %round_trip.1 = (bf16[256,256]{1,0:T(8,128)(2,1)}, bf16[256,2048]{1,0:T(8,128)(2,1)}, f32[16,2,2,512]{3,2,1,0:T(2,128)}) custom-call(bf16[1,2,256,2048]{3,2,1,0:T(8,128)(2,1)} %facets.1, f32[16,2,512]{2,1,0:T(2,128)} %weights.1, s32[2,32]{1,0:T(2,128)} %bitcast.1, s32[16]{0:T(128)} %soff_in.1, s32[1]{0:T(128)S(6)} %copy.7.col_in), custom_call_target="tpu_custom_call" | custom-call | flops 3000000000 | bytes 4000000 | tf_op jit(solution)/shard_map/round_trip/pallas_call | solution.py:344
  65.8 0.0 copy-start
  65.8 1.2 %copy-done = bf16[256,2048]{1,0:T(8,128)(2,1)S(1)} copy-done((bf16[256,2048]{1,0:T(8,128)(2,1)S(1)}, bf16[256,2048]{1,0:T(8,128)(2,1)}, u32[]{:S(2)}) %copy-start) | copy-done | bytes 1048600
  67.0 0.0 copy-start.1
  67.0 0.9 %copy-done.1 = bf16[256,256]{1,0:T(8,128)(2,1)S(1)} copy-done((bf16[256,256]{1,0:T(8,128)(2,1)S(1)}, bf16[256,256]{1,0:T(8,128)(2,1)}, u32[]{:S(2)}) %copy-start.1) | copy-done | bytes 131096
  67.9 0.0 copy-start.2
  67.9 0.9 %copy-done.2 = f32[16,2,2,512]{3,2,1,0:T(2,128)S(1)} copy-done((f32[16,2,2,512]{3,2,1,0:T(2,128)S(1)}, f32[16,2,2,512]{3,2,1,0:T(2,128)}, u32[]{:S(2)}) %copy-start.2) | copy-done | bytes 131096
  68.8 1.7 %correction.1 = (bf16[1,2,256,2048]{3,2,1,0:T(8,128)(2,1)}, f32[16,2,2,512]{3,2,1,0:T(2,128)}) custom-call(bf16[256,256]{1,0:T(8,128)(2,1)S(1)} %copy-done.1, bf16[256,2048]{1,0:T(8,128)(2,1)S(1)} %copy-done, f32[16,2,2,512]{3,2,1,0:T(2,128)S(1)} %copy-done.2), custom_call_target="tpu_custom_call" | custom-call | flops 1000000000 | bytes 3000000 | tf_op jit(solution)/shard_map/correction/pallas_call | solution.py:396
Async XLA Ops:
  65.8 1.2 %copy-start = (bf16[256,2048]{1,0:T(8,128)(2,1)S(1)}, bf16[256,2048]{1,0:T(8,128)(2,1)}, u32[]{:S(2)}) copy-start(bf16[256,2048]{1,0:T(8,128)(2,1)} %get-tuple-element.6.q) | copy-start | bytes 3145732
  67.0 0.9 %copy-start.1 = (bf16[256,256]{1,0:T(8,128)(2,1)S(1)}, bf16[256,256]{1,0:T(8,128)(2,1)}, u32[]{:S(2)}) copy-start(bf16[256,256]{1,0:T(8,128)(2,1)} %get-tuple-element.5.et) | copy-start | bytes 393220
  67.9 0.9 %copy-start.2 = (f32[16,2,2,512]{3,2,1,0:T(2,128)S(1)}, f32[16,2,2,512]{3,2,1,0:T(2,128)}, u32[]{:S(2)}) copy-start(f32[16,2,2,512]{3,2,1,0:T(2,128)} %get-tuple-element.7.spectra_in) | copy-start | bytes 393220

commit v3 on v2

--- a/solution.py
+++ b/solution.py
@@ -62,10 +62,10 @@
 
 def round_trip(
     facets, weights, foff_in, soff_in, col_in,
-    et_out, q_out, spectra,
-    foff, soff, col, x_buf, w_buf, hi_c, hi_s, lo_c, lo_s, p_tab, f_tab, r_tab, perm,
-    a_buf, send1, recv1, send2, mid2, recv2, recv3, win3, rows3, recv4, send5, recv5,
-    small_sem, x_sem, w_sem, sa, ra, s1, r1, s2, r2, sz2, rz2, sz3, rz3, s3, r3, s4, r4, s5, r5,
+    et_hbm, q_hbm, spectra_hbm,
+    et_out, q_out, spectra, foff, soff, col, x_buf, w_buf, hi_c, hi_s, lo_c, lo_s, p_tab, f_tab, r_tab, perm,
+    a_buf, send1, recv1, send2, mid2, ring, got2, recv3, win3, rows3, recv4, send5, recv5,
+    out_sem, small_sem, x_sem, w_sem, sa, ra, s1, r1, s2, r2, sz2, rz2, sz3, rz3, s3, r3, s4, r4, s5, r5,
 ):
     mine = lax.axis_index("facet")
     x = lax.axis_index("half")
@@ -101,7 +101,7 @@
     load_w.start()
 
     barrier = pltpu.get_barrier_semaphore()
-    friends = [across] + [at_x(d) for d in (1, 2, 3)] + [at_slot(q) for q in (1, 2, 3)] + [at_z(d) for d in range(1, 8)]
+    friends = [across] + [at_x(d) for d in (1, 2, 3)] + [at_slot(q) for q in (1, 2, 3)] + [at_z(1), at_z(7)]
     for to in friends:
         pl.semaphore_signal(barrier, inc=1, device_id=to, device_id_type=MESH)
 
@@ -123,6 +123,9 @@
         at = pl.multiple_of(a * 16, 16)
         q_out[pl.ds(at, 16), :] = (hc * lc - hs * ls).astype(BF16)
         q_out[pl.ds(at + M, 16), :] = (-(hs * lc + hc * ls)).astype(BF16)
+
+    store_q = pltpu.make_async_copy(q_out, q_hbm, out_sem.at[0])
+    store_q.start()
 
     turn = foff[1, mine] & (M - 1)
     k, c = iota((2 * M, 2 * M), 0), iota((2 * M, 2 * M), 1)
@@ -193,9 +196,6 @@
         hc, hs = c[a : a + 1], s[a : a + 1]
         f_tab[16 * a : 16 * a + 16, :XM] = (hc * lc - hs * ls).astype(BF16)
         f_tab[16 * a : 16 * a + 16, XM:] = (hs * lc + hc * ls).astype(BF16)
-
-    far = (4, 3, 5, 2, 6, 1, 7)
-    near = (1, 7, 2, 6, 3, 5, 4)
 
     for l in range(PAIR):
         total = recv1[l, 0].astype(F32)
@@ -212,66 +212,115 @@
             remote(send2.at[l, slot_of(q)], mid2.at[l, slot], s2.at[l, q], r2.at[l, q], at_slot(q)).start()
         mid2[l, slot] = send2[l, slot]
 
-    def z2(l, d):
-        return remote(
-            mid2.at[l, :, lax.rem(z + d, 8)], recv2.at[l, z], sz2.at[l, d], rz2.at[l, d], at_z(d)
-        )
-
-    for l in range(PAIR):
-        for q in (1, 2, 3):
-            remote(send2.at[l, slot_of(q)], mid2.at[l, slot_of(q)], s2.at[l, q], r2.at[l, q], at_slot(q)).wait_recv()
-        for d in far:
-            z2(l, d).start()
-
     lane = iota((BLOCK, M), 1)
 
     def tiles_of(f):
         o = foff[1, f]
         return (lax.shift_right_logical(o, 7) + jnp.where(lane < (o & (M - 1)), 1, 0)) & 3
 
+    def hops(l, way):
+        return 4 if l == way else 3
+
+    def on(way, count):
+        return lax.rem(z + (count if way == 0 else 8 - count), 8)
+
+    def onward(way):
+        return at_z(1 if way == 0 else 7)
+
+    chains = [(l, way) for l in range(PAIR) for way in range(2)]
+    own_tiles = [tiles_of((q // 2) * 16 + z * 2 + q % 2) for q in range(4)]
+
+    def placed(l, to_z, part):
+        acc = [jnp.zeros((BLOCK, M), F32) for _ in range(4)]
+        for q in range(4):
+            value = mid2[l, q, to_z, part].astype(F32)
+            acc = [acc[t] + jnp.where(own_tiles[q] == t, value, 0.0) for t in range(4)]
+        return jnp.concatenate(acc, 1)
+
+    def z2(l, way, t):
+        return remote(
+            ring.at[l, way, t], got2.at[l, way, t], sz2.at[4 * l + 2 * way + t // 2, t % 2],
+            rz2.at[4 * l + 2 * way + t // 2, t % 2], onward(way),
+        )
+
+    for t in range(4):
+        for l, way in chains:
+            if t == 0 and way == 0:
+                for q in (1, 2, 3):
+                    remote(
+                        send2.at[l, slot_of(q)], mid2.at[l, slot_of(q)], s2.at[l, q], r2.at[l, q], at_slot(q)
+                    ).wait_recv()
+            if t >= hops(l, way):
+                continue
+            to_z = on(way, hops(l, way) - t)
+            mine_in = [placed(l, to_z, part) for part in range(2)]
+            if t:
+                z2(l, way, t - 1).wait_recv()
+                mine_in = [mine_in[part] + got2[l, way, t - 1, part].astype(F32) for part in range(2)]
+            for part in range(2):
+                ring[l, way, t, part] = mine_in[part].astype(BF16)
+            z2(l, way, t).start()
+
+    def z3(l, way, t):
+        block = recv3.at[l, on(1 - way, t)]
+        return remote(
+            block, block, sz3.at[4 * l + 2 * way + t // 2, t % 2], rz3.at[4 * l + 2 * way + t // 2, t % 2], onward(way)
+        )
+
+    def z3_in(l, way, t):
+        block = recv3.at[l, on(1 - way, t + 1)]
+        return remote(
+            block, block, sz3.at[4 * l + 2 * way + t // 2, t % 2], rz3.at[4 * l + 2 * way + t // 2, t % 2], onward(way)
+        )
+
     load_w.wait()
     for l in range(PAIR):
-        acc = [[jnp.zeros((BLOCK, M), F32) for _ in range(4)] for _ in range(2)]
-        for d in (0,) + near:
-            from_z = lax.rem(z + 8 - d, 8)
-            if d:
-                remote(recv2.at[l, from_z], recv2.at[l, from_z], sz2.at[l, d], rz2.at[l, d], at_z(d)).wait_recv()
-            for q in range(4):
-                tile = tiles_of((q // 2) * 16 + from_z * 2 + q % 2)
-                for part in range(2):
-                    got = (recv2[l, from_z, q, part] if d else mid2[l, q, z, part]).astype(F32)
-                    for t in range(4):
-                        acc[part][t] = acc[part][t] + jnp.where(tile == t, got, 0.0)
-        g = jnp.concatenate([jnp.concatenate(acc[0], 1), jnp.concatenate(acc[1], 1)], 0).astype(BF16)
-        v = dot(g, f_tab[...])
+        g = [placed(l, z, part) for part in range(2)]
+        for way in (1 - l, l):
+            last = hops(l, way) - 1
+            z2(l, way, last).wait_recv()
+            g = [g[part] + got2[l, way, last, part].astype(F32) for part in range(2)]
+        v = dot(jnp.concatenate(g, 0).astype(BF16), f_tab[...])
         weight = w_buf[:, l, :]
         h_real = weight * (v[:BLOCK, :XM] + v[BLOCK:, XM:])
         h_imag = weight * (v[BLOCK:, :XM] - v[:BLOCK, XM:])
         v = dot(jnp.concatenate([h_real, h_imag], 0).astype(BF16), f_tab[...])
         recv3[l, z, 0] = (v[:BLOCK, :XM] - v[BLOCK:, XM:]).astype(BF16)
         recv3[l, z, 1] = (v[BLOCK:, :XM] + v[:BLOCK, XM:]).astype(BF16)
-        for d in far:
-            remote(recv3.at[l, z], recv3.at[l, z], sz3.at[l, d], rz3.at[l, d], at_z(d)).start()
+        for way in range(2):
+            z3(l, way, 0).start()
         spectra[:, l, 0, :] = h_real
         spectra[:, l, 1, :] = h_imag
-
-    for l in range(PAIR):
-        tiles = [tiles_of(lax.rem(low + q // 2, 2) * 16 + z * 2 + lax.rem(core + q % 2, 2)) for q in range(4)]
-        for d in (0,) + near:
-            from_z = lax.rem(z + 8 - d, 8)
-            if d:
-                remote(recv3.at[l, from_z], recv3.at[l, from_z], sz3.at[l, d], rz3.at[l, d], at_z(d)).wait_recv()
-            for part in range(2):
-                whole = recv3[l, from_z, part].astype(F32)
-                cut = [whole[:, M * t : M * t + M] for t in range(4)]
-                for q in range(4):
-                    one = jnp.where(tiles[q] == 1, cut[1], cut[0])
-                    two = jnp.where(tiles[q] == 3, cut[3], cut[2])
-                    one = jnp.where(tiles[q] < 2, one, two).astype(BF16)
-                    if q:
-                        win3[l, q, from_z, part] = one
-                    else:
-                        rows3[l, slot, from_z, part] = one
+    store_s = pltpu.make_async_copy(spectra, spectra_hbm, out_sem.at[1])
+    store_s.start()
+
+    tiles = [tiles_of(lax.rem(low + q // 2, 2) * 16 + z * 2 + lax.rem(core + q % 2, 2)) for q in range(4)]
+
+    def windows(l, from_z):
+        for part in range(2):
+            whole = recv3[l, from_z, part].astype(F32)
+            cut = [whole[:, M * t : M * t + M] for t in range(4)]
+            for q in range(4):
+                one = jnp.where(tiles[q] == 1, cut[1], cut[0])
+                two = jnp.where(tiles[q] == 3, cut[3], cut[2])
+                one = jnp.where(tiles[q] < 2, one, two).astype(BF16)
+                if q:
+                    win3[l, q, from_z, part] = one
+                else:
+                    rows3[l, slot, from_z, part] = one
+
+    for l in range(PAIR):
+        windows(l, z)
+    for t in range(3):
+        for l, way in chains:
+            z3_in(l, way, t).wait_recv()
+            if t + 1 < hops(l, way):
+                z3(l, way, t + 1).start()
+        for l, way in chains:
+            windows(l, on(1 - way, t + 1))
+    for l in range(PAIR):
+        z3_in(l, l, 3).wait_recv()
+        windows(l, on(1 - l, 4))
         for q in (3, 2, 1):
             remote(win3.at[l, q], rows3.at[l, slot], s3.at[l, q], r3.at[l, q], at_slot(q)).start()
 
@@ -299,35 +348,48 @@
     send5[...] = e_there.astype(BF16)
     swap_e = remote(send5, recv5, s5, r5, across)
     swap_e.start()
-    swap_e.wait_recv()
-    e = (e_here + recv5[...].astype(F32)).astype(BF16)
-    et_out[...] = dot(perm[...], e).astype(BF16)
-
-    swap_e.wait_send()
     for l in range(PAIR):
         for d in range(1, 4):
             remote(send1.at[l, d], recv1.at[l, d], s1.at[l, d], r1.at[l, d], at_x(d)).wait_send()
             remote(recv4.at[l, x], recv4.at[l, x], s4.at[l, d], r4.at[l, d], at_x(d)).wait_send()
             remote(send2.at[l, slot_of(d)], mid2.at[l, slot], s2.at[l, d], r2.at[l, d], at_slot(d)).wait_send()
             remote(win3.at[l, d], rows3.at[l, slot], s3.at[l, d], r3.at[l, d], at_slot(d)).wait_send()
-        for d in range(1, 8):
-            z2(l, d).wait_send()
-            remote(recv3.at[l, z], recv3.at[l, z], sz3.at[l, d], rz3.at[l, d], at_z(d)).wait_send()
-
-
-def correction(et, q, spectra_in, out, spectra, buf, sems, sem):
+        for way in range(2):
+            for t in range(hops(l, way)):
+                z2(l, way, t).wait_send()
+                z3(l, way, t).wait_send()
+    store_q.wait()
+    store_s.wait()
+    swap_e.wait_recv()
+    e = (e_here + recv5[...].astype(F32)).astype(BF16)
+    et_out[...] = dot(perm[...], e).astype(BF16)
+    store_e = pltpu.make_async_copy(et_out, et_hbm, out_sem.at[2])
+    store_e.start()
+    swap_e.wait_send()
+    store_e.wait()
+
+
+def correction(et_hbm, q_hbm, spectra_in, out, spectra, et, q, buf, load_sem, sems, sem):
     copy = pltpu.make_async_copy(spectra_in, spectra, sem)
     copy.start()
+    parts = buf.shape[0]
+    width = buf.shape[3]
+    load = pltpu.make_async_copy(et_hbm, et, load_sem.at[parts])
+    load.start()
+    tables = [
+        pltpu.make_async_copy(q_hbm.at[:, pl.ds(width * i, width)], q.at[i], load_sem.at[i]) for i in range(parts)
+    ]
+    for table in tables:
+        table.start()
     gain = 2.0 * math.sqrt(YF / M)
+    load.wait()
     real = et[...]
     imag = jnp.concatenate([real[M:], -real[:M]], 0)
-    parts = buf.shape[0]
-    width = buf.shape[3]
     moves = []
     for i in range(parts):
-        table = q[:, width * i : width * i + width]
-        buf[i, 0] = (dot_t(real, table) * gain).astype(BF16)
-        buf[i, 1] = (dot_t(imag, table) * gain).astype(BF16)
+        tables[i].wait()
+        buf[i, 0] = (dot_t(real, q[i]) * gain).astype(BF16)
+        buf[i, 1] = (dot_t(imag, q[i]) * gain).astype(BF16)
         move = pltpu.make_async_copy(buf.at[i], out.at[0, :, :, pl.ds(width * i, width)], sems.at[i])
         move.start()
         moves.append(move)
@@ -338,7 +400,6 @@
 
 def shards(facets, weights, facet_offsets, subgrid_offsets, column):
     hbm = pl.BlockSpec(memory_space=pl.ANY)
-    vmem = pl.BlockSpec(memory_space=pltpu.VMEM)
     dma = pltpu.SemaphoreType.DMA
     pair_of = lambda *shape: pltpu.VMEM((PAIR, *shape), BF16)
     et, q, spectra = pl.pallas_call(
@@ -349,8 +410,11 @@
             jax.ShapeDtypeStruct((BLOCK, PAIR, 2, XM), F32),
         ),
         in_specs=[hbm] * 5,
-        out_specs=(vmem, vmem, vmem),
+        out_specs=(hbm, hbm, hbm),
         scratch_shapes=[
+            pltpu.VMEM((2 * M, ROWS), BF16),
+            pltpu.VMEM((2 * M, YF), BF16),
+            pltpu.VMEM((BLOCK, PAIR, 2, XM), F32),
             pltpu.SMEM((2, FACETS), jnp.int32),
             pltpu.SMEM((SUBS,), jnp.int32),
             pltpu.SMEM((1,), jnp.int32),
@@ -369,19 +433,20 @@
             pair_of(4, M, 2 * M),
             pair_of(4, 8, 2, BLOCK, M),
             pair_of(4, 8, 2, BLOCK, M),
-            pair_of(8, 4, 2, BLOCK, M),
+            pair_of(2, 4, 2, BLOCK, XM),
+            pair_of(2, 4, 2, BLOCK, XM),
             pair_of(8, 2, BLOCK, XM),
             pair_of(4, 8, 2, BLOCK, M),
             pair_of(4, 8, 2, BLOCK, M),
             pair_of(4, M, 2 * M),
             pltpu.VMEM((2 * M, ROWS), BF16),
             pltpu.VMEM((2 * M, ROWS), BF16),
-            dma((3,)), dma, dma,
+            dma((3,)), dma((3,)), dma, dma,
             dma, dma,
             dma((PAIR, 4)), dma((PAIR, 4)),
             dma((PAIR, 4)), dma((PAIR, 4)),
-            dma((PAIR, 8)), dma((PAIR, 8)),
-            dma((PAIR, 8)), dma((PAIR, 8)),
+            dma((8, 2)), dma((8, 2)),
+            dma((8, 2)), dma((8, 2)),
             dma((PAIR, 4)), dma((PAIR, 4)),
             dma((PAIR, 4)), dma((PAIR, 4)),
             dma, dma,
@@ -399,14 +464,17 @@
             jax.ShapeDtypeStruct((1, 2, ROWS, YF), BF16),
             jax.ShapeDtypeStruct((BLOCK, PAIR, 2, XM), F32),
         ),
-        in_specs=[vmem, vmem, hbm],
+        in_specs=[hbm] * 3,
         out_specs=(hbm, hbm),
         scratch_shapes=[
+            pltpu.VMEM((2 * M, ROWS), BF16),
+            pltpu.VMEM((parts, 2 * M, YF // parts), BF16),
             pltpu.VMEM((parts, 2, ROWS, YF // parts), BF16),
+            dma((parts + 1,)),
             dma((parts,)),
             dma,
         ],
-        compiler_params=pltpu.CompilerParams(vmem_limit_bytes=24 * 2**20),
+        compiler_params=pltpu.CompilerParams(vmem_limit_bytes=VMEM_MIB * 2**20),
         cost_estimate=pl.CostEstimate(flops=10**9, bytes_accessed=3 * 10**6, transcendentals=0),
         name="correction",
     )(et, q, spectra)

time: 70.7 us -> 75.4 us (1.066)
  the two profiles are of different devices: /device:TPU:2 before, /device:TPU:1 now
where the time goes in v3:
time: 75.4 us; the launch traced here: 74.1 us
  Pallas kernels  72.9 us (97%)
  between operations  1.29 us (2%)
    pallas_call x1, Pallas kernels, shards(): pl.pallas_call(round_trip, out_shape=(jax.ShapeDtypeStruct((2 * M, ROWS),...  67.7 us
    pallas_call x1, Pallas kernels, shards(): pl.pallas_call(correction, out_shape=(jax.ShapeDtypeStruct((1, 2, ROWS, Y...  5.16 us

profile of v3, /device:TPU:1, one launch (start us, length us, event | category | flops | bytes accessed | tf_op | source)
XLA Modules:
  0.0 74.1 jit_solution(14129514694834702477)
XLA Ops:
  1.3 67.7 %round_trip.1 = (bf16[256,256]{1,0:T(8,128)(2,1)}, bf16[256,2048]{1,0:T(8,128)(2,1)}, f32[16,2,2,512]{3,2,1,0:T(2,128)}) custom-call(bf16[1,2,256,2048]{3,2,1,0:T(8,128)(2,1)} %facets.1, f32[16,2,512]{2,1,0:T(2,128)} %weights.1, s32[2,32]{1,0:T(2,128)} %bitcast.1, s32[16]{0:T(128)} %soff_in.1, s32[1]{0:T(128)S(6)} %copy.7.col_in), custom_call_target="tpu_custom_call" | custom-call | flops 3000000000 | bytes 4000000 | tf_op jit(solution)/shard_map/round_trip/pallas_call | solution.py:405
  69.0 5.2 %correction.1 = (bf16[1,2,256,2048]{3,2,1,0:T(8,128)(2,1)}, f32[16,2,2,512]{3,2,1,0:T(2,128)}) custom-call(bf16[256,256]{1,0:T(8,128)(2,1)} %get-tuple-element.5.et_hbm, bf16[256,2048]{1,0:T(8,128)(2,1)} %get-tuple-element.6.q_hbm, f32[16,2,2,512]{3,2,1,0:T(2,128)} %get-tuple-element.7.spectra_in), custom_call_target="tpu_custom_call" | custom-call | flops 1000000000 | bytes 3000000 | tf_op jit(solution)/shard_map/correction/pallas_call | solution.py:461

commit v4 on v2

--- a/solution.py
+++ b/solution.py
@@ -16,7 +16,7 @@
 PAIR = 2
 ROWS = 256
 BLOCK = 16
-VMEM_MIB = 60
+VMEM_MIB = 52
 MESH = pl.DeviceIdType.MESH
 F32 = jnp.float32
 BF16 = jnp.bfloat16
@@ -64,8 +64,8 @@
     facets, weights, foff_in, soff_in, col_in,
     et_out, q_out, spectra,
     foff, soff, col, x_buf, w_buf, hi_c, hi_s, lo_c, lo_s, p_tab, f_tab, r_tab, perm,
-    a_buf, send1, recv1, send2, mid2, recv2, recv3, win3, rows3, recv4, send5, recv5,
-    small_sem, x_sem, w_sem, sa, ra, s1, r1, s2, r2, sz2, rz2, sz3, rz3, s3, r3, s4, r4, s5, r5,
+    a_buf, p_own, send1, recv1, send2, recv2, send3, recv3, recv4, send5, recv5,
+    small_sem, x_sem, w_sem, sa, ra, s1, r1, s2, r2, s3, r3, s4, r4, s5, r5,
 ):
     mine = lax.axis_index("facet")
     x = lax.axis_index("half")
@@ -73,19 +73,13 @@
     core = lax.rem(mine, 2)
     z = lax.rem(mine // 2, 8)
     low = mine // 16
-    slot = low * 2 + core
 
     def at_x(d):
         return {"half": lax.rem(x + d, 4)}
 
-    def at_z(d):
-        return {"facet": low * 16 + lax.rem(z + d, 8) * 2 + core}
-
-    def slot_of(q):
-        return lax.rem(low + q // 2, 2) * 2 + lax.rem(core + q % 2, 2)
-
-    def at_slot(q):
-        return {"facet": lax.rem(low + q // 2, 2) * 16 + z * 2 + lax.rem(core + q % 2, 2)}
+    def peer(i, j):
+        dz = 4 + ((i + 1) // 2) * (1 - 2 * lax.rem(i, 2))
+        return lax.rem(low + 1 - j // 2, 2) * 16 + lax.rem(z + dz, 8) * 2 + lax.rem(core + 1 - j % 2, 2)
 
     across = {"sub": 1 - hi}
 
@@ -101,8 +95,13 @@
     load_w.start()
 
     barrier = pltpu.get_barrier_semaphore()
-    friends = [across] + [at_x(d) for d in (1, 2, 3)] + [at_slot(q) for q in (1, 2, 3)] + [at_z(d) for d in range(1, 8)]
+    friends = [across] + [at_x(d) for d in (1, 2, 3)]
     for to in friends:
+        pl.semaphore_signal(barrier, inc=1, device_id=to, device_id_type=MESH)
+
+    @pl.loop(1, FACETS)
+    def _(i):
+        to = {"facet": lax.rem(mine + i, FACETS)}
         pl.semaphore_signal(barrier, inc=1, device_id=to, device_id_type=MESH)
 
     y = iota((8, YF), 1)
@@ -139,7 +138,7 @@
     ).astype(BF16)
     a_buf[hi] = dot(a_both, perm[...]).astype(BF16)
 
-    pl.semaphore_wait(barrier, len(friends))
+    pl.semaphore_wait(barrier, len(friends) + FACETS - 1)
     swap_a = remote(a_buf.at[hi], a_buf.at[hi], sa, ra, across)
     swap_a.start()
 
@@ -161,9 +160,13 @@
                 p_tab[b, u, 16 * a : 16 * a + 16, :] = real[:, ROWS * b : ROWS * b + ROWS]
                 p_tab[b, u, M + 16 * a : M + 16 * a + 16, :] = imag[:, ROWS * b : ROWS * b + ROWS]
 
+    @pl.loop(0, 2 * 4)
+    def _(u):
+        p_own[u] = dot(p_tab[hi, u], a_buf[hi])
+
     def partial(l, to_x):
         u = 2 * to_x + l
-        v = dot(p_tab[0, u], a_buf[0]) + dot(p_tab[1, u], a_buf[1])
+        v = p_own[u] + dot(p_tab[1 - hi, u], a_buf[1 - hi])
         return jnp.concatenate([v[:M, :M] - v[M:, M:], v[:M, M:] + v[M:, :M]], 1).astype(BF16)
 
     swap_a.wait()
@@ -178,9 +181,7 @@
     lc, ls = cis(iota((16, M), 0) * place & (XM - 1), XM)
     lc, ls = lc * scale, ls * scale
     place = (foff[0, mine] + iota((32, M), 1)) & (XM - 1)
-    i = iota((32, M), 0)
-    block = (i & 16) + 2 * (i & 7) + (lax.shift_right_logical(i, 3) & 1)
-    hc, hs = cis(16 * block * place & (XM - 1), XM)
+    hc, hs = cis(16 * iota((32, M), 0) * place & (XM - 1), XM)
     for a in range(32):
         c, s = hc[a : a + 1], hs[a : a + 1]
         r_tab[16 * a : 16 * a + 16, :M] = (c * lc - s * ls).astype(BF16)
@@ -194,8 +195,18 @@
         f_tab[16 * a : 16 * a + 16, :XM] = (hc * lc - hs * ls).astype(BF16)
         f_tab[16 * a : 16 * a + 16, XM:] = (hs * lc + hc * ls).astype(BF16)
 
-    far = (4, 3, 5, 2, 6, 1, 7)
-    near = (1, 7, 2, 6, 3, 5, 4)
+    def bulk(send, recv, l, ssem, rsem):
+        some = pl.ds(0, FACETS - 1)
+        return remote(send.at[l, some], recv.at[l, some], ssem.at[l], rsem.at[l], {"facet": peer(0, 0)})
+
+    def to_all(action):
+        @pl.loop(0, 7)
+        def _(i):
+            for j in range(4):
+                action(peer(i, j))
+
+        for j in range(3):
+            action(peer(7, j))
 
     for l in range(PAIR):
         total = recv1[l, 0].astype(F32)
@@ -206,22 +217,10 @@
         cr, ci = total[:, :M], total[:, M:]
         both = jnp.concatenate([jnp.concatenate([cr, ci], 1), jnp.concatenate([ci, -cr], 1)], 0)
         kk = dot(r_tab[...], both).astype(BF16)
-        send2[l, :, :, 0] = kk[:, :M].reshape(4, 8, BLOCK, M)
-        send2[l, :, :, 1] = kk[:, M:].reshape(4, 8, BLOCK, M)
-        for q in (3, 2, 1):
-            remote(send2.at[l, slot_of(q)], mid2.at[l, slot], s2.at[l, q], r2.at[l, q], at_slot(q)).start()
-        mid2[l, slot] = send2[l, slot]
-
-    def z2(l, d):
-        return remote(
-            mid2.at[l, :, lax.rem(z + d, 8)], recv2.at[l, z], sz2.at[l, d], rz2.at[l, d], at_z(d)
-        )
-
-    for l in range(PAIR):
-        for q in (1, 2, 3):
-            remote(send2.at[l, slot_of(q)], mid2.at[l, slot_of(q)], s2.at[l, q], r2.at[l, q], at_slot(q)).wait_recv()
-        for d in far:
-            z2(l, d).start()
+        send2[l, :, 0] = kk[:, :M].reshape(FACETS, BLOCK, M)
+        send2[l, :, 1] = kk[:, M:].reshape(FACETS, BLOCK, M)
+        to_all(lambda f: remote(send2.at[l, f], recv2.at[l, mine], s2.at[l], r2.at[l], {"facet": f}).start())
+        recv2[l, mine] = send2[l, mine]
 
     lane = iota((BLOCK, M), 1)
 
@@ -231,88 +230,84 @@
 
     load_w.wait()
     for l in range(PAIR):
-        acc = [[jnp.zeros((BLOCK, M), F32) for _ in range(4)] for _ in range(2)]
-        for d in (0,) + near:
-            from_z = lax.rem(z + 8 - d, 8)
-            if d:
-                remote(recv2.at[l, from_z], recv2.at[l, from_z], sz2.at[l, d], rz2.at[l, d], at_z(d)).wait_recv()
-            for q in range(4):
-                tile = tiles_of((q // 2) * 16 + from_z * 2 + q % 2)
-                for part in range(2):
-                    got = (recv2[l, from_z, q, part] if d else mid2[l, q, z, part]).astype(F32)
-                    for t in range(4):
-                        acc[part][t] = acc[part][t] + jnp.where(tile == t, got, 0.0)
-        g = jnp.concatenate([jnp.concatenate(acc[0], 1), jnp.concatenate(acc[1], 1)], 0).astype(BF16)
+        bulk(send2, recv2, l, s2, r2).wait_recv()
+
+        def gather(i, acc):
+            for f in (2 * i, 2 * i + 1):
+                tile = tiles_of(f)
+                got = [recv2[l, f, part].astype(F32) for part in range(2)]
+                acc = tuple(
+                    acc[4 * part + t] + jnp.where(tile == t, got[part], 0.0) for part in range(2) for t in range(4)
+                )
+            return acc
+
+        acc = lax.fori_loop(0, FACETS // 2, gather, (jnp.zeros((BLOCK, M), F32),) * 8)
+        g = jnp.concatenate([jnp.concatenate(acc[:4], 1), jnp.concatenate(acc[4:], 1)], 0).astype(BF16)
         v = dot(g, f_tab[...])
         weight = w_buf[:, l, :]
         h_real = weight * (v[:BLOCK, :XM] + v[BLOCK:, XM:])
         h_imag = weight * (v[BLOCK:, :XM] - v[:BLOCK, XM:])
         v = dot(jnp.concatenate([h_real, h_imag], 0).astype(BF16), f_tab[...])
-        recv3[l, z, 0] = (v[:BLOCK, :XM] - v[BLOCK:, XM:]).astype(BF16)
-        recv3[l, z, 1] = (v[BLOCK:, :XM] + v[:BLOCK, XM:]).astype(BF16)
-        for d in far:
-            remote(recv3.at[l, z], recv3.at[l, z], sz3.at[l, d], rz3.at[l, d], at_z(d)).start()
+        space = [v[:BLOCK, :XM] - v[BLOCK:, XM:], v[BLOCK:, :XM] + v[:BLOCK, XM:]]
+
+        def window(f):
+            tile = tiles_of(f)
+            for part in range(2):
+                cut = [space[part][:, M * t : M * t + M] for t in range(4)]
+                one = jnp.where(tile == 1, cut[1], cut[0])
+                two = jnp.where(tile == 3, cut[3], cut[2])
+                send3[l, f, part] = jnp.where(tile < 2, one, two).astype(BF16)
+
+        def window_out(f):
+            window(f)
+            remote(send3.at[l, f], recv3.at[l, mine], s3.at[l], r3.at[l], {"facet": f}).start()
+
+        to_all(window_out)
+        window(mine)
+        recv3[l, mine] = send3[l, mine]
         spectra[:, l, 0, :] = h_real
         spectra[:, l, 1, :] = h_imag
 
     for l in range(PAIR):
-        tiles = [tiles_of(lax.rem(low + q // 2, 2) * 16 + z * 2 + lax.rem(core + q % 2, 2)) for q in range(4)]
-        for d in (0,) + near:
-            from_z = lax.rem(z + 8 - d, 8)
-            if d:
-                remote(recv3.at[l, from_z], recv3.at[l, from_z], sz3.at[l, d], rz3.at[l, d], at_z(d)).wait_recv()
-            for part in range(2):
-                whole = recv3[l, from_z, part].astype(F32)
-                cut = [whole[:, M * t : M * t + M] for t in range(4)]
-                for q in range(4):
-                    one = jnp.where(tiles[q] == 1, cut[1], cut[0])
-                    two = jnp.where(tiles[q] == 3, cut[3], cut[2])
-                    one = jnp.where(tiles[q] < 2, one, two).astype(BF16)
-                    if q:
-                        win3[l, q, from_z, part] = one
-                    else:
-                        rows3[l, slot, from_z, part] = one
-        for q in (3, 2, 1):
-            remote(win3.at[l, q], rows3.at[l, slot], s3.at[l, q], r3.at[l, q], at_slot(q)).start()
-
-    e_here = e_there = None
-    for l in range(PAIR):
-        for q in (1, 2, 3):
-            remote(win3.at[l, q], rows3.at[l, slot_of(q)], s3.at[l, q], r3.at[l, q], at_slot(q)).wait_recv()
-        rows = jnp.concatenate([rows3[l, :, :, 0].reshape(XM, M), rows3[l, :, :, 1].reshape(XM, M)], 1)
+        bulk(send3, recv3, l, s3, r3).wait_recv()
+        rows = jnp.concatenate([recv3[l, :, 0].reshape(XM, M), recv3[l, :, 1].reshape(XM, M)], 1)
         u = dot_t(rows, r_tab[...])
         recv4[l, x] = jnp.concatenate([u[:M, :M] - u[M:, M:], u[M:, :M] + u[:M, M:]], 1).astype(BF16)
         for d in (2, 1, 3):
             remote(recv4.at[l, x], recv4.at[l, x], s4.at[l, d], r4.at[l, d], at_x(d)).start()
 
+    def spread(l, d, block):
+        from_x = lax.rem(x + 4 - d, 4)
+        v = recv4[l, from_x]
+        v = jnp.concatenate([v, jnp.concatenate([v[:, M:], -v[:, :M]], 1)], 0)
+        return dot(v, p_tab[block, 2 * from_x + l])
+
+    e_there = e_here = None
     for l in range(PAIR):
         for d in (0, 1, 3, 2):
             from_x = lax.rem(x + 4 - d, 4)
             if d:
                 remote(recv4.at[l, from_x], recv4.at[l, from_x], s4.at[l, d], r4.at[l, d], at_x(d)).wait_recv()
-            v = recv4[l, from_x]
-            v = jnp.concatenate([v, jnp.concatenate([v[:, M:], -v[:, :M]], 1)], 0)
-            there = dot(v, p_tab[1 - hi, 2 * from_x + l])
-            here = dot(v, p_tab[hi, 2 * from_x + l])
+            there = spread(l, d, 1 - hi)
             e_there = there if e_there is None else e_there + there
-            e_here = here if e_here is None else e_here + here
+            if l == 0:
+                here = spread(l, d, hi)
+                e_here = here if e_here is None else e_here + here
     send5[...] = e_there.astype(BF16)
     swap_e = remote(send5, recv5, s5, r5, across)
     swap_e.start()
+    for d in (0, 1, 3, 2):
+        e_here = e_here + spread(1, d, hi)
+    for l in range(PAIR):
+        bulk(send2, recv2, l, s2, r2).wait_send()
+        bulk(send3, recv3, l, s3, r3).wait_send()
+        for d in range(1, 4):
+            remote(send1.at[l, d], recv1.at[l, d], s1.at[l, d], r1.at[l, d], at_x(d)).wait_send()
+            remote(recv4.at[l, x], recv4.at[l, x], s4.at[l, d], r4.at[l, d], at_x(d)).wait_send()
     swap_e.wait_recv()
     e = (e_here + recv5[...].astype(F32)).astype(BF16)
     et_out[...] = dot(perm[...], e).astype(BF16)
-
     swap_e.wait_send()
-    for l in range(PAIR):
-        for d in range(1, 4):
-            remote(send1.at[l, d], recv1.at[l, d], s1.at[l, d], r1.at[l, d], at_x(d)).wait_send()
-            remote(recv4.at[l, x], recv4.at[l, x], s4.at[l, d], r4.at[l, d], at_x(d)).wait_send()
-            remote(send2.at[l, slot_of(d)], mid2.at[l, slot], s2.at[l, d], r2.at[l, d], at_slot(d)).wait_send()
-            remote(win3.at[l, d], rows3.at[l, slot], s3.at[l, d], r3.at[l, d], at_slot(d)).wait_send()
-        for d in range(1, 8):
-            z2(l, d).wait_send()
-            remote(recv3.at[l, z], recv3.at[l, z], sz3.at[l, d], rz3.at[l, d], at_z(d)).wait_send()
 
 
 def correction(et, q, spectra_in, out, spectra, buf, sems, sem):
@@ -337,7 +332,8 @@
 
 
 def shards(facets, weights, facet_offsets, subgrid_offsets, column):
-    hbm = pl.BlockSpec(memory_space=pl.ANY)
+    hbm = pl.BlockSpec(memory_space=pltpu.HBM)
+    anywhere = pl.BlockSpec(memory_space=pl.ANY)
     vmem = pl.BlockSpec(memory_space=pltpu.VMEM)
     dma = pltpu.SemaphoreType.DMA
     pair_of = lambda *shape: pltpu.VMEM((PAIR, *shape), BF16)
@@ -365,24 +361,21 @@
             pltpu.VMEM((XM, 2 * M), BF16),
             pltpu.VMEM((2 * M, 2 * M), BF16),
             pltpu.VMEM((2, ROWS, 2 * M), BF16),
+            pltpu.VMEM((8, 2 * M, 2 * M), F32),
             pair_of(4, M, 2 * M),
             pair_of(4, M, 2 * M),
-            pair_of(4, 8, 2, BLOCK, M),
-            pair_of(4, 8, 2, BLOCK, M),
-            pair_of(8, 4, 2, BLOCK, M),
-            pair_of(8, 2, BLOCK, XM),
-            pair_of(4, 8, 2, BLOCK, M),
-            pair_of(4, 8, 2, BLOCK, M),
+            pair_of(FACETS, 2, BLOCK, M),
+            pair_of(FACETS, 2, BLOCK, M),
+            pair_of(FACETS, 2, BLOCK, M),
+            pair_of(FACETS, 2, BLOCK, M),
             pair_of(4, M, 2 * M),
             pltpu.VMEM((2 * M, ROWS), BF16),
             pltpu.VMEM((2 * M, ROWS), BF16),
             dma((3,)), dma, dma,
             dma, dma,
             dma((PAIR, 4)), dma((PAIR, 4)),
-            dma((PAIR, 4)), dma((PAIR, 4)),
-            dma((PAIR, 8)), dma((PAIR, 8)),
-            dma((PAIR, 8)), dma((PAIR, 8)),
-            dma((PAIR, 4)), dma((PAIR, 4)),
+            dma((PAIR,)), dma((PAIR,)),
+            dma((PAIR,)), dma((PAIR,)),
             dma((PAIR, 4)), dma((PAIR, 4)),
             dma, dma,
         ],
@@ -399,7 +392,7 @@
             jax.ShapeDtypeStruct((1, 2, ROWS, YF), BF16),
             jax.ShapeDtypeStruct((BLOCK, PAIR, 2, XM), F32),
         ),
-        in_specs=[vmem, vmem, hbm],
+        in_specs=[vmem, vmem, anywhere],
         out_specs=(hbm, hbm),
         scratch_shapes=[
             pltpu.VMEM((parts, 2, ROWS, YF // parts), BF16),

time: 70.7 us -> 62.7 us (0.89)
  the two profiles are of different devices: /device:TPU:2 before, /device:TPU:1 now
where the time goes in v4:
time: 62.7 us; the launch traced here: 62.5 us
  Pallas kernels  59.1 us (94%)
  local copies, waits for them, and re-layouts  2.17 us (3%)
  between operations  1.3 us (2%)
    pallas_call x1, Pallas kernels, shards(): pl.pallas_call(round_trip, out_shape=(jax.ShapeDtypeStruct((2 * M, ROWS),...  57.4 us
    unnamed x6, local copies, waits for them, and re-layouts  2.17 us
    pallas_call x1, Pallas kernels, shards(): pl.pallas_call(correction, out_shape=(jax.ShapeDtypeStruct((1, 2, ROWS, Y...  1.68 us

profile of v4, /device:TPU:1, one launch (start us, length us, event | category | flops | bytes accessed | tf_op | source)
XLA Modules:
  0.0 62.5 jit_solution(4658896957284051292)
XLA Ops:
  1.3 0.0 copy-start
  1.3 0.8 %copy-done = f32[16,2,512]{2,1,0:T(2,128)S(1)} copy-done((f32[16,2,512]{2,1,0:T(2,128)S(1)}, f32[16,2,512]{2,1,0:T(2,128)}, u32[]{:S(2)}) %copy-start) | copy-done | bytes 65560
  2.1 0.0 copy-start.1
  2.1 0.7 %copy-done.1 = s32[32,2]{0,1:T(2,128)S(1)} copy-done((s32[32,2]{0,1:T(2,128)S(1)}, s32[32,2]{0,1:T(2,128)}, u32[]{:S(2)}) %copy-start.1) | copy-done | bytes 280
  2.8 0.0 copy-start.2
  2.8 0.7 %copy-done.2 = s32[16]{0:T(128)S(1)} copy-done((s32[16]{0:T(128)S(1)}, s32[16]{0:T(128)}, u32[]{:S(2)}) %copy-start.2) | copy-done | bytes 88
  3.5 57.4 %round_trip.1 = (bf16[256,256]{1,0:T(8,128)(2,1)S(1)}, bf16[256,2048]{1,0:T(8,128)(2,1)S(1)}, f32[16,2,2,512]{3,2,1,0:T(2,128)S(1)}) custom-call(bf16[1,2,256,2048]{3,2,1,0:T(8,128)(2,1)} %facets.1, f32[16,2,512]{2,1,0:T(2,128)S(1)} %copy-done, s32[2,32]{1,0:T(2,128)S(1)} %bitcast.1, s32[16]{0:T(128)S(1)} %copy-done.2, s32[1]{0:T(128)S(6)} %copy.7.col_in), custom_call_target="tpu_custom_call" | custom-call | flops 3000000000 | bytes 4000000 | tf_op jit(solution)/shard_map/round_trip/pallas_call | solution.py:340
  60.8 1.7 %correction.1 = (bf16[1,2,256,2048]{3,2,1,0:T(8,128)(2,1)}, f32[16,2,2,512]{3,2,1,0:T(2,128)}) custom-call(bf16[256,256]{1,0:T(8,128)(2,1)S(1)} %get-tuple-element.5.et, bf16[256,2048]{1,0:T(8,128)(2,1)S(1)} %get-tuple-element.6.q, f32[16,2,2,512]{3,2,1,0:T(2,128)S(1)} %get-tuple-element.7.spectra_in), custom_call_target="tpu_custom_call" | custom-call | flops 1000000000 | bytes 3000000 | tf_op jit(solution)/shard_map/correction/pallas_call | solution.py:389
Async XLA Ops:
  1.3 0.8 %copy-start = (f32[16,2,512]{2,1,0:T(2,128)S(1)}, f32[16,2,512]{2,1,0:T(2,128)}, u32[]{:S(2)}) copy-start(f32[16,2,512]{2,1,0:T(2,128)} %weights.1) | copy-start | bytes 196612
  2.1 0.7 %copy-start.1 = (s32[32,2]{0,1:T(2,128)S(1)}, s32[32,2]{0,1:T(2,128)}, u32[]{:S(2)}) copy-start(s32[32,2]{0,1:T(2,128)} %param.7) | copy-start | bytes 772
  2.8 0.7 %copy-start.2 = (s32[16]{0:T(128)S(1)}, s32[16]{0:T(128)}, u32[]{:S(2)}) copy-start(s32[16]{0:T(128)} %soff_in.1) | copy-start | bytes 196

commit v5 on v4

--- a/solution.py
+++ b/solution.py
@@ -16,7 +16,8 @@
 PAIR = 2
 ROWS = 256
 BLOCK = 16
-VMEM_MIB = 52
+PIECES = 4
+VMEM_MIB = 60
 MESH = pl.DeviceIdType.MESH
 F32 = jnp.float32
 BF16 = jnp.bfloat16
@@ -62,10 +63,10 @@
 
 def round_trip(
     facets, weights, foff_in, soff_in, col_in,
-    et_out, q_out, spectra,
-    foff, soff, col, x_buf, w_buf, hi_c, hi_s, lo_c, lo_s, p_tab, f_tab, r_tab, perm,
-    a_buf, p_own, send1, recv1, send2, recv2, send3, recv3, recv4, send5, recv5,
-    small_sem, x_sem, w_sem, sa, ra, s1, r1, s2, r2, s3, r3, s4, r4, s5, r5,
+    et_hbm, q_hbm, spectra_hbm,
+    et_out, q_out, q_turned, spectra, foff, soff, col, x_buf, w_buf, hi_c, hi_s, lo_c, lo_s, p_tab, p_wide, f_tab, r_tab, perm,
+    a_low, a_high, kept, send1, recv1, send2, recv2, send3, recv3, recv4, recv4y, send5, recv5,
+    out_sem, small_sem, x_sem, w_sem, sa, ra, s1, r1, s2, r2, s3, r3, s4, r4, s5, r5,
 ):
     mine = lax.axis_index("facet")
     x = lax.axis_index("half")
@@ -89,8 +90,13 @@
     ]
     for copy in smalls:
         copy.start()
-    load = pltpu.make_async_copy(facets.at[0], x_buf, x_sem)
-    load.start()
+    width = YF // PIECES
+    loads = [
+        pltpu.make_async_copy(facets.at[0, :, :, pl.ds(width * i, width)], x_buf.at[i], x_sem.at[i])
+        for i in range(PIECES)
+    ]
+    for load in loads:
+        load.start()
     load_w = pltpu.make_async_copy(weights, w_buf, w_sem)
     load_w.start()
 
@@ -124,23 +130,36 @@
         q_out[pl.ds(at + M, 16), :] = (-(hs * lc + hc * ls)).astype(BF16)
 
     turn = foff[1, mine] & (M - 1)
-    k, c = iota((2 * M, 2 * M), 0), iota((2 * M, 2 * M), 1)
-    same = ((k & (M - 1)) == ((c - turn) & (M - 1))) & ((k < M) == (c < M))
+    r, c = iota((2 * M, 2 * M), 0), iota((2 * M, 2 * M), 1)
+    k = lax.shift_right_logical(c, 7) * 64 + (c & 63)
+    same = ((r & (M - 1)) == ((k - turn) & (M - 1))) & (lax.shift_right_logical(r, 7) == (lax.shift_right_logical(c, 6) & 1))
     perm[...] = jnp.where(same, 1.0, 0.0).astype(BF16)
 
-    load.wait()
-    q = q_out[...]
     over = (((1,), (1,)), ((), ()))
-    from_real = lax.dot_general(x_buf[0], q, over, preferred_element_type=F32)
-    from_imag = lax.dot_general(x_buf[1], q, over, preferred_element_type=F32)
+    from_real = from_imag = None
+    for i, load in enumerate(loads):
+        load.wait()
+        q = q_out[:, width * i : width * i + width]
+        real = lax.dot_general(x_buf[i, 0], q, over, preferred_element_type=F32)
+        imag = lax.dot_general(x_buf[i, 1], q, over, preferred_element_type=F32)
+        from_real = real if i == 0 else from_real + real
+        from_imag = imag if i == 0 else from_imag + imag
     a_both = jnp.concatenate(
         [from_real[:, :M] - from_imag[:, M:], from_real[:, M:] + from_imag[:, :M]], 1
     ).astype(BF16)
-    a_buf[hi] = dot(a_both, perm[...]).astype(BF16)
+    a_both = dot(a_both, perm[...]).astype(BF16)
+    a_low[hi] = a_both[:, :M]
+    a_high[x] = a_both[:, M:]
 
     pl.semaphore_wait(barrier, len(friends) + FACETS - 1)
-    swap_a = remote(a_buf.at[hi], a_buf.at[hi], sa, ra, across)
-    swap_a.start()
+
+    def swap_a(d):
+        if d:
+            return remote(a_high.at[x], a_high.at[x], sa.at[d], ra.at[d], at_x(d))
+        return remote(a_low.at[hi], a_low.at[hi], sa.at[0], ra.at[0], across)
+
+    for d in (2, 0, 1, 3):
+        swap_a(d).start()
 
     first = x * (2 * ROWS)
     pos = first + iota((16, 2 * ROWS), 1)
@@ -160,21 +179,69 @@
                 p_tab[b, u, 16 * a : 16 * a + 16, :] = real[:, ROWS * b : ROWS * b + ROWS]
                 p_tab[b, u, M + 16 * a : M + 16 * a + 16, :] = imag[:, ROWS * b : ROWS * b + ROWS]
 
-    @pl.loop(0, 2 * 4)
-    def _(u):
-        p_own[u] = dot(p_tab[hi, u], a_buf[hi])
-
-    def partial(l, to_x):
+    for b in range(4):
+        first_b = (2 * b + hi) * ROWS
+        c, s = cis(iota((16, ROWS), 0) * (first_b + iota((16, ROWS), 1)) & (YF - 1), YF)
+        w = taper(first_b + iota((1, ROWS), 1))
+        lc_b, ls_b = c * w, s * w
+
+        @pl.loop(0, 4)
+        def _(u):
+            freq = (soff[4 * x + u] + 16 * iota((8, ROWS), 0)) & (YF - 1)
+            hc, hs = cis(freq * (first_b + iota((8, ROWS), 1)) & (YF - 1), YF)
+            for a in range(8):
+                c, s = hc[a : a + 1], hs[a : a + 1]
+                p_wide[b, u, 16 * a : 16 * a + 16, :] = (c * lc_b - s * ls_b).astype(BF16)
+                p_wide[b, u, M + 16 * a : M + 16 * a + 16, :] = (-(s * lc_b + c * ls_b)).astype(BF16)
+
+    left = iota((M, M), 1) < 64
+
+    def complex_sum(v):
+        turned = pltpu.roll(v[M:], 64, 1)
+        return v[:M] + jnp.where(left, -turned, turned)
+
+    for u in range(8):
+        kept[u] = dot(p_tab[hi, u], a_low[hi])
+    for u in range(4):
+        kept[8 + u] = dot(p_wide[x, u], a_high[x])
+
+    def partial_low(l, to_x):
         u = 2 * to_x + l
-        v = p_own[u] + dot(p_tab[1 - hi, u], a_buf[1 - hi])
-        return jnp.concatenate([v[:M, :M] - v[M:, M:], v[:M, M:] + v[M:, :M]], 1).astype(BF16)
-
-    swap_a.wait()
-    for l in range(PAIR):
-        for d in (2, 1, 3):
-            send1[l, d] = partial(l, lax.rem(x + d, 4))
-            remote(send1.at[l, d], recv1.at[l, d], s1.at[l, d], r1.at[l, d], at_x(d)).start()
-        recv1[l, 0] = partial(l, x)
+        return complex_sum(kept[u] + dot(p_tab[1 - hi, u], a_low[1 - hi]))
+
+    def partial_high(l, to_hi):
+        u = 2 * to_hi + l
+        v = kept[8 + u]
+        for d in (1, 3, 2):
+            v = v + dot(p_wide[lax.rem(x + 4 - d, 4), u], a_high[lax.rem(x + 4 - d, 4)])
+        return complex_sum(v)
+
+    def sum1(l, d):
+        return remote(send1.at[l, d], recv1.at[l, d], s1.at[l, d], r1.at[l, d], at_x(d) if d else across)
+
+    for d in (0, 1, 3, 2):
+        if d:
+            block = a_high.at[lax.rem(x + 4 - d, 4)]
+            remote(block, block, sa.at[d], ra.at[d], at_x(d)).wait_recv()
+        else:
+            remote(a_low.at[1 - hi], a_low.at[1 - hi], sa.at[0], ra.at[0], across).wait_recv()
+            for d_low in (2, 1, 3):
+                send1[0, d_low] = partial_low(0, lax.rem(x + d_low, 4)).astype(BF16)
+                sum1(0, d_low).start()
+    own = []
+    for l in range(PAIR):
+        send1[l, 0] = partial_high(l, 1 - hi).astype(BF16)
+        sum1(l, 0).start()
+        if l:
+            for d in (2, 1, 3):
+                send1[l, d] = partial_low(l, lax.rem(x + d, 4)).astype(BF16)
+                sum1(l, d).start()
+    for l in range(PAIR):
+        own.append((partial_low(l, x), partial_high(l, hi)))
+
+    q_turned[...] = dot_t(perm[...], q_out[...]).astype(BF16)
+    store_q = pltpu.make_async_copy(q_turned, q_hbm, out_sem.at[0])
+    store_q.start()
 
     scale = 1.0 / math.sqrt(XM)
     place = (foff[0, mine] + iota((16, M), 1)) & (XM - 1)
@@ -209,12 +276,15 @@
             action(peer(7, j))
 
     for l in range(PAIR):
-        total = recv1[l, 0].astype(F32)
-        for d in (1, 3, 2):
-            remote(send1.at[l, d], recv1.at[l, d], s1.at[l, d], r1.at[l, d], at_x(d)).wait_recv()
-            total = total + recv1[l, d].astype(F32)
-        total = total.astype(BF16)
-        cr, ci = total[:, :M], total[:, M:]
+        low_k, high_k = own[l]
+        for d in (0, 1, 3, 2):
+            sum1(l, d).wait_recv()
+            if d:
+                low_k = low_k + recv1[l, d].astype(F32)
+            else:
+                high_k = high_k + recv1[l, d].astype(F32)
+        cr = jnp.where(left, low_k, pltpu.roll(high_k, 64, 1)).astype(BF16)
+        ci = jnp.where(left, pltpu.roll(low_k, 64, 1), high_k).astype(BF16)
         both = jnp.concatenate([jnp.concatenate([cr, ci], 1), jnp.concatenate([ci, -cr], 1)], 0)
         kk = dot(r_tab[...], both).astype(BF16)
         send2[l, :, 0] = kk[:, :M].reshape(FACETS, BLOCK, M)
@@ -267,74 +337,120 @@
         recv3[l, mine] = send3[l, mine]
         spectra[:, l, 0, :] = h_real
         spectra[:, l, 1, :] = h_imag
+    store_s = pltpu.make_async_copy(spectra, spectra_hbm, out_sem.at[1])
+    store_s.start()
+
+    def send4(l, d):
+        if d:
+            return remote(recv4.at[l, x], recv4.at[l, x], s4.at[l, d], r4.at[l, d], at_x(d))
+        return remote(recv4y.at[l, hi], recv4y.at[l, hi], s4.at[l, 0], r4.at[l, 0], across)
+
+    def swap_e(d):
+        return remote(send5.at[d], recv5.at[d], s5.at[d], r5.at[d], at_x(d) if d else across)
 
     for l in range(PAIR):
         bulk(send3, recv3, l, s3, r3).wait_recv()
         rows = jnp.concatenate([recv3[l, :, 0].reshape(XM, M), recv3[l, :, 1].reshape(XM, M)], 1)
         u = dot_t(rows, r_tab[...])
-        recv4[l, x] = jnp.concatenate([u[:M, :M] - u[M:, M:], u[M:, :M] + u[:M, M:]], 1).astype(BF16)
-        for d in (2, 1, 3):
-            remote(recv4.at[l, x], recv4.at[l, x], s4.at[l, d], r4.at[l, d], at_x(d)).start()
-
-    def spread(l, d, block):
-        from_x = lax.rem(x + 4 - d, 4)
-        v = recv4[l, from_x]
-        v = jnp.concatenate([v, jnp.concatenate([v[:, M:], -v[:, :M]], 1)], 0)
-        return dot(v, p_tab[block, 2 * from_x + l])
-
-    e_there = e_here = None
+        d_both = jnp.concatenate([u[:M, :M] - u[M:, M:], u[M:, :M] + u[:M, M:]], 1).astype(BF16)
+        recv4[l, x] = d_both[:64]
+        recv4y[l, hi] = d_both[64:]
+        for d in (2, 0, 1, 3):
+            send4(l, d).start()
+
+    def twice(v):
+        return jnp.concatenate([v, jnp.concatenate([v[:, M:], -v[:, :M]], 1)], 0)
+
+    def add(total, term):
+        return term if total is None else total + term
+
+    low_e, high_e = [None, None], [None] * 4
     for l in range(PAIR):
         for d in (0, 1, 3, 2):
             from_x = lax.rem(x + 4 - d, 4)
             if d:
-                remote(recv4.at[l, from_x], recv4.at[l, from_x], s4.at[l, d], r4.at[l, d], at_x(d)).wait_recv()
-            there = spread(l, d, 1 - hi)
-            e_there = there if e_there is None else e_there + there
+                block = recv4.at[l, from_x]
+                remote(block, block, s4.at[l, d], r4.at[l, d], at_x(d)).wait_recv()
+            else:
+                block = recv4y.at[l, 1 - hi]
+                remote(block, block, s4.at[l, d], r4.at[l, d], across).wait_recv()
+                for near_hi in (hi, 1 - hi):
+                    v = twice(recv4y[l, near_hi])
+                    for e in (2, 1, 3) if l else (2, 1, 3, 0):
+                        high_e[e] = add(high_e[e], dot(v, p_wide[lax.rem(x + e, 4), 2 * near_hi + l]))
+                if l:
+                    for e in (2, 1, 3):
+                        send5[e] = high_e[e].astype(BF16)
+                        swap_e(e).start()
+            v = twice(recv4[l, from_x])
+            low_e[1] = add(low_e[1], dot(v, p_tab[1 - hi, 2 * from_x + l]))
             if l == 0:
-                here = spread(l, d, hi)
-                e_here = here if e_here is None else e_here + here
-    send5[...] = e_there.astype(BF16)
-    swap_e = remote(send5, recv5, s5, r5, across)
-    swap_e.start()
-    for d in (0, 1, 3, 2):
-        e_here = e_here + spread(1, d, hi)
+                low_e[0] = add(low_e[0], dot(v, p_tab[hi, 2 * from_x]))
+    send5[0] = low_e[1].astype(BF16)
+    swap_e(0).start()
+    for d in range(4):
+        from_x = lax.rem(x + 4 - d, 4)
+        low_e[0] = low_e[0] + dot(twice(recv4[1, from_x]), p_tab[hi, 2 * from_x + 1])
+    for near_hi in range(2):
+        high_e[0] = high_e[0] + dot(twice(recv4y[1, near_hi]), p_wide[x, 2 * near_hi + 1])
     for l in range(PAIR):
         bulk(send2, recv2, l, s2, r2).wait_send()
         bulk(send3, recv3, l, s3, r3).wait_send()
-        for d in range(1, 4):
-            remote(send1.at[l, d], recv1.at[l, d], s1.at[l, d], r1.at[l, d], at_x(d)).wait_send()
-            remote(recv4.at[l, x], recv4.at[l, x], s4.at[l, d], r4.at[l, d], at_x(d)).wait_send()
-    swap_e.wait_recv()
-    e = (e_here + recv5[...].astype(F32)).astype(BF16)
-    et_out[...] = dot(perm[...], e).astype(BF16)
-    swap_e.wait_send()
-
-
-def correction(et, q, spectra_in, out, spectra, buf, sems, sem):
-    copy = pltpu.make_async_copy(spectra_in, spectra, sem)
-    copy.start()
-    gain = 2.0 * math.sqrt(YF / M)
-    real = et[...]
-    imag = jnp.concatenate([real[M:], -real[:M]], 0)
+        for d in range(4):
+            sum1(l, d).wait_send()
+            send4(l, d).wait_send()
+    for d in range(4):
+        swap_a(d).wait_send()
+    store_q.wait()
+    store_s.wait()
+    low_k, high_k = low_e[0], high_e[0]
+    for d in (1, 3, 2, 0):
+        swap_e(d).wait_recv()
+        if d:
+            high_k = high_k + recv5[d].astype(F32)
+        else:
+            low_k = low_k + recv5[d].astype(F32)
+    et_out[...] = jnp.concatenate([low_k, high_k], 0).astype(BF16)
+    store_e = pltpu.make_async_copy(et_out, et_hbm, out_sem.at[2])
+    store_e.start()
+    for d in range(4):
+        swap_e(d).wait_send()
+    store_e.wait()
+
+
+def correction(et_hbm, q_hbm, spectra_in, out, spectra_out, et, q, spectra, buf, load_sem, store_sem):
     parts = buf.shape[0]
     width = buf.shape[3]
+    load = pltpu.make_async_copy(et_hbm, et, load_sem.at[parts])
+    load.start()
+    tables = [
+        pltpu.make_async_copy(q_hbm.at[:, pl.ds(width * i, width)], q.at[i], load_sem.at[i]) for i in range(parts)
+    ]
+    for table in tables:
+        table.start()
+    load_s = pltpu.make_async_copy(spectra_in, spectra, load_sem.at[parts + 1])
+    load_s.start()
+    gain = 2.0 * math.sqrt(YF / M)
+    load.wait()
+    real = et[...]
+    imag = jnp.concatenate([real[64:128], -real[:64], real[192:], -real[128:192]], 0)
     moves = []
     for i in range(parts):
-        table = q[:, width * i : width * i + width]
-        buf[i, 0] = (dot_t(real, table) * gain).astype(BF16)
-        buf[i, 1] = (dot_t(imag, table) * gain).astype(BF16)
-        move = pltpu.make_async_copy(buf.at[i], out.at[0, :, :, pl.ds(width * i, width)], sems.at[i])
-        move.start()
-        moves.append(move)
+        tables[i].wait()
+        buf[i, 0] = (dot_t(real, q[i]) * gain).astype(BF16)
+        buf[i, 1] = (dot_t(imag, q[i]) * gain).astype(BF16)
+        moves.append(pltpu.make_async_copy(buf.at[i], out.at[0, :, :, pl.ds(width * i, width)], store_sem.at[i]))
+        moves[-1].start()
+        if i == 0:
+            load_s.wait()
+            moves.append(pltpu.make_async_copy(spectra, spectra_out, store_sem.at[parts]))
+            moves[-1].start()
     for move in moves:
         move.wait()
-    copy.wait()
 
 
 def shards(facets, weights, facet_offsets, subgrid_offsets, column):
     hbm = pl.BlockSpec(memory_space=pltpu.HBM)
-    anywhere = pl.BlockSpec(memory_space=pl.ANY)
-    vmem = pl.BlockSpec(memory_space=pltpu.VMEM)
     dma = pltpu.SemaphoreType.DMA
     pair_of = lambda *shape: pltpu.VMEM((PAIR, *shape), BF16)
     et, q, spectra = pl.pallas_call(
@@ -345,39 +461,46 @@
             jax.ShapeDtypeStruct((BLOCK, PAIR, 2, XM), F32),
         ),
         in_specs=[hbm] * 5,
-        out_specs=(vmem, vmem, vmem),
+        out_specs=(hbm, hbm, hbm),
         scratch_shapes=[
+            pltpu.VMEM((2 * M, ROWS), BF16),
+            pltpu.VMEM((2 * M, YF), BF16),
+            pltpu.VMEM((2 * M, YF), BF16),
+            pltpu.VMEM((BLOCK, PAIR, 2, XM), F32),
             pltpu.SMEM((2, FACETS), jnp.int32),
             pltpu.SMEM((SUBS,), jnp.int32),
             pltpu.SMEM((1,), jnp.int32),
-            pltpu.VMEM((2, ROWS, YF), BF16),
+            pltpu.VMEM((PIECES, 2, ROWS, YF // PIECES), BF16),
             pltpu.VMEM((BLOCK, PAIR, XM), F32),
             pltpu.VMEM((8, YF), F32),
             pltpu.VMEM((8, YF), F32),
             pltpu.VMEM((16, YF), F32),
             pltpu.VMEM((16, YF), F32),
             pltpu.VMEM((2, 8, 2 * M, ROWS), BF16),
+            pltpu.VMEM((4, 4, 2 * M, ROWS), BF16),
             pltpu.VMEM((XM, 2 * XM), BF16),
             pltpu.VMEM((XM, 2 * M), BF16),
             pltpu.VMEM((2 * M, 2 * M), BF16),
-            pltpu.VMEM((2, ROWS, 2 * M), BF16),
-            pltpu.VMEM((8, 2 * M, 2 * M), F32),
-            pair_of(4, M, 2 * M),
-            pair_of(4, M, 2 * M),
+            pltpu.VMEM((2, ROWS, M), BF16),
+            pltpu.VMEM((4, ROWS, M), BF16),
+            pltpu.VMEM((12, 2 * M, M), F32),
+            pair_of(4, M, M),
+            pair_of(4, M, M),
             pair_of(FACETS, 2, BLOCK, M),
             pair_of(FACETS, 2, BLOCK, M),
             pair_of(FACETS, 2, BLOCK, M),
             pair_of(FACETS, 2, BLOCK, M),
-            pair_of(4, M, 2 * M),
-            pltpu.VMEM((2 * M, ROWS), BF16),
-            pltpu.VMEM((2 * M, ROWS), BF16),
-            dma((3,)), dma, dma,
-            dma, dma,
+            pair_of(4, 64, 2 * M),
+            pair_of(2, 64, 2 * M),
+            pltpu.VMEM((4, M, ROWS), BF16),
+            pltpu.VMEM((4, M, ROWS), BF16),
+            dma((3,)), dma((3,)), dma((PIECES,)), dma,
+            dma((4,)), dma((4,)),
             dma((PAIR, 4)), dma((PAIR, 4)),
             dma((PAIR,)), dma((PAIR,)),
             dma((PAIR,)), dma((PAIR,)),
             dma((PAIR, 4)), dma((PAIR, 4)),
-            dma, dma,
+            dma((4,)), dma((4,)),
         ],
         compiler_params=pltpu.CompilerParams(
             collective_id=0, has_side_effects=True, vmem_limit_bytes=VMEM_MIB * 2**20
@@ -392,14 +515,17 @@
             jax.ShapeDtypeStruct((1, 2, ROWS, YF), BF16),
             jax.ShapeDtypeStruct((BLOCK, PAIR, 2, XM), F32),
         ),
-        in_specs=[vmem, vmem, anywhere],
+        in_specs=[hbm] * 3,
         out_specs=(hbm, hbm),
         scratch_shapes=[
+            pltpu.VMEM((2 * M, ROWS), BF16),
+            pltpu.VMEM((parts, 2 * M, YF // parts), BF16),
+            pltpu.VMEM((BLOCK, PAIR, 2, XM), F32),
             pltpu.VMEM((parts, 2, ROWS, YF // parts), BF16),
-            dma((parts,)),
-            dma,
+            dma((parts + 2,)),
+            dma((parts + 1,)),
         ],
-        compiler_params=pltpu.CompilerParams(vmem_limit_bytes=24 * 2**20),
+        compiler_params=pltpu.CompilerParams(vmem_limit_bytes=VMEM_MIB * 2**20),
         cost_estimate=pl.CostEstimate(flops=10**9, bytes_accessed=3 * 10**6, transcendentals=0),
         name="correction",
     )(et, q, spectra)

time: 62.7 us -> 58.3 us (0.930)
  Pallas kernels: 59.1 us -> 56.9 us
  local copies, waits for them, and re-layouts: 2.17 us -> 0 us
    pallas_call x1, Pallas kernels: 57.4 us -> 53.8 us  [shards(): pl.pallas_call(round_trip, out_shape=(jax.ShapeDtypeStruct((2 * M, ROWS),...]
    unnamed x6 -> x0, local copies, waits for them, and re-layouts: 2.17 us -> none
    pallas_call x1, Pallas kernels: 1.68 us -> 3.15 us  [shards(): pl.pallas_call(correction, out_shape=(jax.ShapeDtypeStruct((1, 2, ROWS, Y...]
where the time goes in v5:
time: 58.3 us; the launch traced here: 58.2 us
  Pallas kernels  56.9 us (98%)
  between operations  1.29 us (2%)
    pallas_call x1, Pallas kernels, shards(): pl.pallas_call(round_trip, out_shape=(jax.ShapeDtypeStruct((2 * M, ROWS),...  53.8 us
    pallas_call x1, Pallas kernels, shards(): pl.pallas_call(correction, out_shape=(jax.ShapeDtypeStruct((1, 2, ROWS, Y...  3.15 us

profile of v5, /device:TPU:1, one launch (start us, length us, event | category | flops | bytes accessed | tf_op | source)
XLA Modules:
  0.0 58.2 jit_solution(14992112223557182809)
XLA Ops:
  1.3 53.8 %round_trip.1 = (bf16[256,256]{1,0:T(8,128)(2,1)}, bf16[256,2048]{1,0:T(8,128)(2,1)}, f32[16,2,2,512]{3,2,1,0:T(2,128)}) custom-call(bf16[1,2,256,2048]{3,2,1,0:T(8,128)(2,1)} %facets.1, f32[16,2,512]{2,1,0:T(2,128)} %weights.1, s32[2,32]{1,0:T(2,128)} %bitcast.1, s32[16]{0:T(128)} %soff_in.1, s32[1]{0:T(128)S(6)} %copy.7.col_in), custom_call_target="tpu_custom_call" | custom-call | flops 3000000000 | bytes 4000000 | tf_op jit(solution)/shard_map/round_trip/pallas_call | solution.py:456
  55.1 3.2 %correction.1 = (bf16[1,2,256,2048]{3,2,1,0:T(8,128)(2,1)}, f32[16,2,2,512]{3,2,1,0:T(2,128)}) custom-call(bf16[256,256]{1,0:T(8,128)(2,1)} %get-tuple-element.5.et_hbm, bf16[256,2048]{1,0:T(8,128)(2,1)} %get-tuple-element.6.q_hbm, f32[16,2,2,512]{3,2,1,0:T(2,128)} %get-tuple-element.7.spectra_in), custom_call_target="tpu_custom_call" | custom-call | flops 1000000000 | bytes 3000000 | tf_op jit(solution)/shard_map/correction/pallas_call | solution.py:512

commit v6 on v5

--- a/solution.py
+++ b/solution.py
@@ -17,7 +17,7 @@
 ROWS = 256
 BLOCK = 16
 PIECES = 4
-VMEM_MIB = 60
+VMEM_MIB = 52
 MESH = pl.DeviceIdType.MESH
 F32 = jnp.float32
 BF16 = jnp.bfloat16
@@ -62,11 +62,11 @@
 
 
 def round_trip(
-    facets, weights, foff_in, soff_in, col_in,
-    et_hbm, q_hbm, spectra_hbm,
-    et_out, q_out, q_turned, spectra, foff, soff, col, x_buf, w_buf, hi_c, hi_s, lo_c, lo_s, p_tab, p_wide, f_tab, r_tab, perm,
+    facets, weights, offsets_in,
+    et_out, q_turned, spectra,
+    q_out, offsets, x_buf, w_buf, hi_c, hi_s, lo_c, lo_s, p_tab, p_wide, f_tab, r_tab, perm,
     a_low, a_high, kept, send1, recv1, send2, recv2, send3, recv3, recv4, recv4y, send5, recv5,
-    out_sem, small_sem, x_sem, w_sem, sa, ra, s1, r1, s2, r2, s3, r3, s4, r4, s5, r5,
+    small_sem, x_sem, w_sem, sa, ra, s1, r1, s2, r2, s3, r3, s4, r4, s5, r5,
 ):
     mine = lax.axis_index("facet")
     x = lax.axis_index("half")
@@ -78,18 +78,14 @@
     def at_x(d):
         return {"half": lax.rem(x + d, 4)}
 
-    def peer(i, j):
+    def peer(i, dy, dc):
         dz = 4 + ((i + 1) // 2) * (1 - 2 * lax.rem(i, 2))
-        return lax.rem(low + 1 - j // 2, 2) * 16 + lax.rem(z + dz, 8) * 2 + lax.rem(core + 1 - j % 2, 2)
+        return lax.rem(low + dy, 2) * 16 + lax.rem(z + dz, 8) * 2 + lax.rem(core + dc, 2)
 
     across = {"sub": 1 - hi}
 
-    smalls = [
-        pltpu.make_async_copy(src, dst, small_sem.at[i])
-        for i, (src, dst) in enumerate([(col_in, col), (foff_in, foff), (soff_in, soff)])
-    ]
-    for copy in smalls:
-        copy.start()
+    load_o = pltpu.make_async_copy(offsets_in, offsets, small_sem)
+    load_o.start()
     width = YF // PIECES
     loads = [
         pltpu.make_async_copy(facets.at[0, :, :, pl.ds(width * i, width)], x_buf.at[i], x_sem.at[i])
@@ -115,9 +111,8 @@
     w = taper(iota((1, YF), 1))
     lo_c[...] = c * w
     lo_s[...] = s * w
-    for copy in smalls:
-        copy.wait()
-    c, s = cis(((col[0] + 16 * iota((8, YF), 0)) & (YF - 1)) * y & (YF - 1), YF)
+    load_o.wait()
+    c, s = cis(((offsets[3, 0] + 16 * iota((8, YF), 0)) & (YF - 1)) * y & (YF - 1), YF)
     hi_c[...] = c
     hi_s[...] = s
 
@@ -129,7 +124,7 @@
         q_out[pl.ds(at, 16), :] = (hc * lc - hs * ls).astype(BF16)
         q_out[pl.ds(at + M, 16), :] = (-(hs * lc + hc * ls)).astype(BF16)
 
-    turn = foff[1, mine] & (M - 1)
+    turn = offsets[1, mine] & (M - 1)
     r, c = iota((2 * M, 2 * M), 0), iota((2 * M, 2 * M), 1)
     k = lax.shift_right_logical(c, 7) * 64 + (c & 63)
     same = ((r & (M - 1)) == ((k - turn) & (M - 1))) & (lax.shift_right_logical(r, 7) == (lax.shift_right_logical(c, 6) & 1))
@@ -169,7 +164,7 @@
 
     @pl.loop(0, 2 * 4)
     def _(u):
-        freq = (soff[4 * (u // 2) + 2 * hi + lax.rem(u, 2)] + 16 * iota((8, 2 * ROWS), 0)) & (YF - 1)
+        freq = (offsets[2, 4 * (u // 2) + 2 * hi + lax.rem(u, 2)] + 16 * iota((8, 2 * ROWS), 0)) & (YF - 1)
         hc, hs = cis(freq * (first + iota((8, 2 * ROWS), 1)) & (YF - 1), YF)
         for a in range(8):
             c, s = hc[a : a + 1], hs[a : a + 1]
@@ -187,7 +182,7 @@
 
         @pl.loop(0, 4)
         def _(u):
-            freq = (soff[4 * x + u] + 16 * iota((8, ROWS), 0)) & (YF - 1)
+            freq = (offsets[2, 4 * x + u] + 16 * iota((8, ROWS), 0)) & (YF - 1)
             hc, hs = cis(freq * (first_b + iota((8, ROWS), 1)) & (YF - 1), YF)
             for a in range(8):
                 c, s = hc[a : a + 1], hs[a : a + 1]
@@ -240,14 +235,12 @@
         own.append((partial_low(l, x), partial_high(l, hi)))
 
     q_turned[...] = dot_t(perm[...], q_out[...]).astype(BF16)
-    store_q = pltpu.make_async_copy(q_turned, q_hbm, out_sem.at[0])
-    store_q.start()
 
     scale = 1.0 / math.sqrt(XM)
-    place = (foff[0, mine] + iota((16, M), 1)) & (XM - 1)
+    place = (offsets[0, mine] + iota((16, M), 1)) & (XM - 1)
     lc, ls = cis(iota((16, M), 0) * place & (XM - 1), XM)
     lc, ls = lc * scale, ls * scale
-    place = (foff[0, mine] + iota((32, M), 1)) & (XM - 1)
+    place = (offsets[0, mine] + iota((32, M), 1)) & (XM - 1)
     hc, hs = cis(16 * iota((32, M), 0) * place & (XM - 1), XM)
     for a in range(32):
         c, s = hc[a : a + 1], hs[a : a + 1]
@@ -264,16 +257,17 @@
 
     def bulk(send, recv, l, ssem, rsem):
         some = pl.ds(0, FACETS - 1)
-        return remote(send.at[l, some], recv.at[l, some], ssem.at[l], rsem.at[l], {"facet": peer(0, 0)})
+        return remote(send.at[l, some], recv.at[l, some], ssem.at[l], rsem.at[l], {"facet": peer(0, 0, 0)})
 
     def to_all(action):
-        @pl.loop(0, 7)
-        def _(i):
-            for j in range(4):
-                action(peer(i, j))
-
-        for j in range(3):
-            action(peer(7, j))
+        for dc in (1, 0):
+
+            @pl.loop(0, 7 + dc)
+            def _(i):
+                for dy in (1, 0):
+                    action(peer(i, dy, dc))
+
+        action(peer(7, 1, 0))
 
     for l in range(PAIR):
         low_k, high_k = own[l]
@@ -295,7 +289,7 @@
     lane = iota((BLOCK, M), 1)
 
     def tiles_of(f):
-        o = foff[1, f]
+        o = offsets[1, f]
         return (lax.shift_right_logical(o, 7) + jnp.where(lane < (o & (M - 1)), 1, 0)) & 3
 
     load_w.wait()
@@ -337,8 +331,6 @@
         recv3[l, mine] = send3[l, mine]
         spectra[:, l, 0, :] = h_real
         spectra[:, l, 1, :] = h_imag
-    store_s = pltpu.make_async_copy(spectra, spectra_hbm, out_sem.at[1])
-    store_s.start()
 
     def send4(l, d):
         if d:
@@ -401,8 +393,6 @@
             send4(l, d).wait_send()
     for d in range(4):
         swap_a(d).wait_send()
-    store_q.wait()
-    store_s.wait()
     low_k, high_k = low_e[0], high_e[0]
     for d in (1, 3, 2, 0):
         swap_e(d).wait_recv()
@@ -411,48 +401,40 @@
         else:
             low_k = low_k + recv5[d].astype(F32)
     et_out[...] = jnp.concatenate([low_k, high_k], 0).astype(BF16)
-    store_e = pltpu.make_async_copy(et_out, et_hbm, out_sem.at[2])
-    store_e.start()
     for d in range(4):
         swap_e(d).wait_send()
-    store_e.wait()
-
-
-def correction(et_hbm, q_hbm, spectra_in, out, spectra_out, et, q, spectra, buf, load_sem, store_sem):
+
+
+def correction(et, q, spectra_in, out, spectra_out, buf, sems):
     parts = buf.shape[0]
     width = buf.shape[3]
-    load = pltpu.make_async_copy(et_hbm, et, load_sem.at[parts])
-    load.start()
-    tables = [
-        pltpu.make_async_copy(q_hbm.at[:, pl.ds(width * i, width)], q.at[i], load_sem.at[i]) for i in range(parts)
-    ]
-    for table in tables:
-        table.start()
-    load_s = pltpu.make_async_copy(spectra_in, spectra, load_sem.at[parts + 1])
-    load_s.start()
+    moves = [pltpu.make_async_copy(spectra_in, spectra_out, sems.at[parts])]
+    moves[0].start()
     gain = 2.0 * math.sqrt(YF / M)
-    load.wait()
     real = et[...]
     imag = jnp.concatenate([real[64:128], -real[:64], real[192:], -real[128:192]], 0)
-    moves = []
     for i in range(parts):
-        tables[i].wait()
-        buf[i, 0] = (dot_t(real, q[i]) * gain).astype(BF16)
-        buf[i, 1] = (dot_t(imag, q[i]) * gain).astype(BF16)
-        moves.append(pltpu.make_async_copy(buf.at[i], out.at[0, :, :, pl.ds(width * i, width)], store_sem.at[i]))
+        table = q[:, width * i : width * i + width]
+        buf[i, 0] = (dot_t(real, table) * gain).astype(BF16)
+        buf[i, 1] = (dot_t(imag, table) * gain).astype(BF16)
+        moves.append(pltpu.make_async_copy(buf.at[i], out.at[0, :, :, pl.ds(width * i, width)], sems.at[i]))
         moves[-1].start()
-        if i == 0:
-            load_s.wait()
-            moves.append(pltpu.make_async_copy(spectra, spectra_out, store_sem.at[parts]))
-            moves[-1].start()
     for move in moves:
         move.wait()
 
 
 def shards(facets, weights, facet_offsets, subgrid_offsets, column):
     hbm = pl.BlockSpec(memory_space=pltpu.HBM)
+    anywhere = pl.BlockSpec(memory_space=pl.ANY)
+    vmem = pl.BlockSpec(memory_space=pltpu.VMEM)
     dma = pltpu.SemaphoreType.DMA
     pair_of = lambda *shape: pltpu.VMEM((PAIR, *shape), BF16)
+    zero = jnp.int32(0)
+    offsets = (
+        lax.pad(facet_offsets.T, zero, [(0, 2, 0), (0, 0, 0)])
+        + lax.pad(subgrid_offsets[None], zero, [(2, 1, 0), (0, FACETS - SUBS, 0)])
+        + lax.pad(column[None], zero, [(3, 0, 0), (0, FACETS - 1, 0)])
+    )
     et, q, spectra = pl.pallas_call(
         round_trip,
         out_shape=(
@@ -460,16 +442,11 @@
             jax.ShapeDtypeStruct((2 * M, YF), BF16),
             jax.ShapeDtypeStruct((BLOCK, PAIR, 2, XM), F32),
         ),
-        in_specs=[hbm] * 5,
-        out_specs=(hbm, hbm, hbm),
+        in_specs=[hbm] * 3,
+        out_specs=(vmem, vmem, vmem),
         scratch_shapes=[
-            pltpu.VMEM((2 * M, ROWS), BF16),
             pltpu.VMEM((2 * M, YF), BF16),
-            pltpu.VMEM((2 * M, YF), BF16),
-            pltpu.VMEM((BLOCK, PAIR, 2, XM), F32),
-            pltpu.SMEM((2, FACETS), jnp.int32),
-            pltpu.SMEM((SUBS,), jnp.int32),
-            pltpu.SMEM((1,), jnp.int32),
+            pltpu.SMEM((4, FACETS), jnp.int32),
             pltpu.VMEM((PIECES, 2, ROWS, YF // PIECES), BF16),
             pltpu.VMEM((BLOCK, PAIR, XM), F32),
             pltpu.VMEM((8, YF), F32),
@@ -494,7 +471,7 @@
             pair_of(2, 64, 2 * M),
             pltpu.VMEM((4, M, ROWS), BF16),
             pltpu.VMEM((4, M, ROWS), BF16),
-            dma((3,)), dma((3,)), dma((PIECES,)), dma,
+            dma, dma((PIECES,)), dma,
             dma((4,)), dma((4,)),
             dma((PAIR, 4)), dma((PAIR, 4)),
             dma((PAIR,)), dma((PAIR,)),
@@ -507,7 +484,7 @@
         ),
         cost_estimate=pl.CostEstimate(flops=3 * 10**9, bytes_accessed=4 * 10**6, transcendentals=0),
         name="round_trip",
-    )(facets, weights, facet_offsets.T, subgrid_offsets, column)
+    )(facets, weights, offsets)
     parts = 4
     update, spectra = pl.pallas_call(
         correction,
@@ -515,17 +492,13 @@
             jax.ShapeDtypeStruct((1, 2, ROWS, YF), BF16),
             jax.ShapeDtypeStruct((BLOCK, PAIR, 2, XM), F32),
         ),
-        in_specs=[hbm] * 3,
+        in_specs=[vmem, vmem, anywhere],
         out_specs=(hbm, hbm),
         scratch_shapes=[
-            pltpu.VMEM((2 * M, ROWS), BF16),
-            pltpu.VMEM((parts, 2 * M, YF // parts), BF16),
-            pltpu.VMEM((BLOCK, PAIR, 2, XM), F32),
             pltpu.VMEM((parts, 2, ROWS, YF // parts), BF16),
-            dma((parts + 2,)),
             dma((parts + 1,)),
         ],
-        compiler_params=pltpu.CompilerParams(vmem_limit_bytes=VMEM_MIB * 2**20),
+        compiler_params=pltpu.CompilerParams(vmem_limit_bytes=24 * 2**20),
         cost_estimate=pl.CostEstimate(flops=10**9, bytes_accessed=3 * 10**6, transcendentals=0),
         name="correction",
     )(et, q, spectra)

time: 58.3 us -> 57.5 us (0.986)
  the two profiles are of different devices: /device:TPU:1 before, /device:TPU:8 now
where the time goes in v6:
time: 57.5 us; the launch traced here: 57.4 us
  Pallas kernels  54.5 us (95%)
  between operations  1.29 us (2%)
  local copies, waits for them, and re-layouts  0.84 us (1%)
  other arithmetic  0.71 us (1%)
    pallas_call x1, Pallas kernels, shards(): pl.pallas_call(round_trip, out_shape=(jax.ShapeDtypeStruct((2 * M, ROWS),...  52.9 us
    pallas_call x1, Pallas kernels, shards(): pl.pallas_call(correction, out_shape=(jax.ShapeDtypeStruct((1, 2, ROWS, Y...  1.68 us

profile of v6, /device:TPU:8, one launch (start us, length us, event | category | flops | bytes accessed | tf_op | source)
XLA Modules:
  0.0 57.4 jit_solution(1278118769160462693)
XLA Ops:
  1.3 0.7 %pad_add_fusion.offsets_in = s32[4,32]{1,0:T(4,128)S(1)} fusion(s32[1,1]{1,0:T(1,128)} %bitcast.3, s32[1,16]{1,0:T(1,128)} %bitcast.5, s32[2,32]{1,0:T(2,128)} %bitcast.4), kind=kLoop, calls=%fused_computation | loop fusion | flops 256 | bytes 836 | tf_op jit(solution)/shard_map/add | solution.py:434
  2.0 0.0 copy-start
  2.0 0.8 %copy-done = f32[16,2,512]{2,1,0:T(2,128)S(1)} copy-done((f32[16,2,512]{2,1,0:T(2,128)S(1)}, f32[16,2,512]{2,1,0:T(2,128)}, u32[]{:S(2)}) %copy-start) | copy-done | bytes 65560
  2.8 52.9 %round_trip.1 = (bf16[256,256]{1,0:T(8,128)(2,1)S(1)}, bf16[256,2048]{1,0:T(8,128)(2,1)S(1)}, f32[16,2,2,512]{3,2,1,0:T(2,128)S(1)}) custom-call(bf16[1,2,256,2048]{3,2,1,0:T(8,128)(2,1)} %facets.1, f32[16,2,512]{2,1,0:T(2,128)S(1)} %copy-done, s32[4,32]{1,0:T(4,128)S(1)} %pad_add_fusion.offsets_in), custom_call_target="tpu_custom_call" | custom-call | flops 3000000000 | bytes 4000000 | tf_op jit(solution)/shard_map/round_trip/pallas_call | solution.py:438
  55.7 1.7 %correction.1 = (bf16[1,2,256,2048]{3,2,1,0:T(8,128)(2,1)}, f32[16,2,2,512]{3,2,1,0:T(2,128)}) custom-call(bf16[256,256]{1,0:T(8,128)(2,1)S(1)} %get-tuple-element.5.et, bf16[256,2048]{1,0:T(8,128)(2,1)S(1)} %get-tuple-element.6.q, f32[16,2,2,512]{3,2,1,0:T(2,128)S(1)} %get-tuple-element.7.spectra_in), custom_call_target="tpu_custom_call" | custom-call | flops 1000000000 | bytes 3000000 | tf_op jit(solution)/shard_map/correction/pallas_call | solution.py:489
Async XLA Ops:
  2.0 0.8 %copy-start = (f32[16,2,512]{2,1,0:T(2,128)S(1)}, f32[16,2,512]{2,1,0:T(2,128)}, u32[]{:S(2)}) copy-start(f32[16,2,512]{2,1,0:T(2,128)} %weights.1) | copy-start | bytes 196612

commit v7 on v6

--- a/solution.py
+++ b/solution.py
@@ -160,7 +160,7 @@
     pos = first + iota((16, 2 * ROWS), 1)
     c, s = cis(iota((16, 2 * ROWS), 0) * pos & (YF - 1), YF)
     w = taper(first + iota((1, 2 * ROWS), 1))
-    lc, ls = c * w, s * w
+    lc, ls, lc_less, ls_less = c * w, s * w, c * -w, s * -w
 
     @pl.loop(0, 2 * 4)
     def _(u):
@@ -169,7 +169,7 @@
         for a in range(8):
             c, s = hc[a : a + 1], hs[a : a + 1]
             real = (c * lc - s * ls).astype(BF16)
-            imag = (-(s * lc + c * ls)).astype(BF16)
+            imag = (s * lc_less + c * ls_less).astype(BF16)
             for b in range(2):
                 p_tab[b, u, 16 * a : 16 * a + 16, :] = real[:, ROWS * b : ROWS * b + ROWS]
                 p_tab[b, u, M + 16 * a : M + 16 * a + 16, :] = imag[:, ROWS * b : ROWS * b + ROWS]
@@ -178,7 +178,7 @@
         first_b = (2 * b + hi) * ROWS
         c, s = cis(iota((16, ROWS), 0) * (first_b + iota((16, ROWS), 1)) & (YF - 1), YF)
         w = taper(first_b + iota((1, ROWS), 1))
-        lc_b, ls_b = c * w, s * w
+        lc_b, ls_b, lc_less_b, ls_less_b = c * w, s * w, c * -w, s * -w
 
         @pl.loop(0, 4)
         def _(u):
@@ -187,7 +187,7 @@
             for a in range(8):
                 c, s = hc[a : a + 1], hs[a : a + 1]
                 p_wide[b, u, 16 * a : 16 * a + 16, :] = (c * lc_b - s * ls_b).astype(BF16)
-                p_wide[b, u, M + 16 * a : M + 16 * a + 16, :] = (-(s * lc_b + c * ls_b)).astype(BF16)
+                p_wide[b, u, M + 16 * a : M + 16 * a + 16, :] = (s * lc_less_b + c * ls_less_b).astype(BF16)
 
     left = iota((M, M), 1) < 64
 
@@ -259,15 +259,16 @@
         some = pl.ds(0, FACETS - 1)
         return remote(send.at[l, some], recv.at[l, some], ssem.at[l], rsem.at[l], {"facet": peer(0, 0, 0)})
 
-    def to_all(action):
-        for dc in (1, 0):
+    def to_all(action, first=1):
+        for dc in (first, 1 - first):
 
             @pl.loop(0, 7 + dc)
             def _(i):
                 for dy in (1, 0):
                     action(peer(i, dy, dc))
 
-        action(peer(7, 1, 0))
+            if dc == 0:
+                action(peer(7, 1, 0))
 
     for l in range(PAIR):
         low_k, high_k = own[l]
@@ -283,7 +284,7 @@
         kk = dot(r_tab[...], both).astype(BF16)
         send2[l, :, 0] = kk[:, :M].reshape(FACETS, BLOCK, M)
         send2[l, :, 1] = kk[:, M:].reshape(FACETS, BLOCK, M)
-        to_all(lambda f: remote(send2.at[l, f], recv2.at[l, mine], s2.at[l], r2.at[l], {"facet": f}).start())
+        to_all(lambda f: remote(send2.at[l, f], recv2.at[l, mine], s2.at[l], r2.at[l], {"facet": f}).start(), 1 - l)
         recv2[l, mine] = send2[l, mine]
 
     lane = iota((BLOCK, M), 1)
@@ -326,7 +327,7 @@
             window(f)
             remote(send3.at[l, f], recv3.at[l, mine], s3.at[l], r3.at[l], {"facet": f}).start()
 
-        to_all(window_out)
+        to_all(window_out, 1 - l)
         window(mine)
         recv3[l, mine] = send3[l, mine]
         spectra[:, l, 0, :] = h_real

time: 57.5 us -> 57.4 us (level)
  the two profiles are of different devices: /device:TPU:8 before, /device:TPU:1 now
where the time goes in v7:
time: 57.4 us; the launch traced here: 57.3 us
  Pallas kernels  54.5 us (95%)
  between operations  1.29 us (2%)
  local copies, waits for them, and re-layouts  0.84 us (1%)
  other arithmetic  0.71 us (1%)
    pallas_call x1, Pallas kernels, shards(): pl.pallas_call(round_trip, out_shape=(jax.ShapeDtypeStruct((2 * M, ROWS),...  52.8 us
    pallas_call x1, Pallas kernels, shards(): pl.pallas_call(correction, out_shape=(jax.ShapeDtypeStruct((1, 2, ROWS, Y...  1.68 us

profile of v7, /device:TPU:1, one launch (start us, length us, event | category | flops | bytes accessed | tf_op | source)
XLA Modules:
  0.0 57.3 jit_solution(3014658570547921503)
XLA Ops:
  1.3 0.7 %pad_add_fusion.offsets_in = s32[4,32]{1,0:T(4,128)S(1)} fusion(s32[1,1]{1,0:T(1,128)} %bitcast.3, s32[1,16]{1,0:T(1,128)} %bitcast.5, s32[2,32]{1,0:T(2,128)} %bitcast.4), kind=kLoop, calls=%fused_computation | loop fusion | flops 256 | bytes 836 | tf_op jit(solution)/shard_map/add | solution.py:435
  2.0 0.0 copy-start
  2.0 0.8 %copy-done = f32[16,2,512]{2,1,0:T(2,128)S(1)} copy-done((f32[16,2,512]{2,1,0:T(2,128)S(1)}, f32[16,2,512]{2,1,0:T(2,128)}, u32[]{:S(2)}) %copy-start) | copy-done | bytes 65560
  2.8 52.8 %round_trip.1 = (bf16[256,256]{1,0:T(8,128)(2,1)S(1)}, bf16[256,2048]{1,0:T(8,128)(2,1)S(1)}, f32[16,2,2,512]{3,2,1,0:T(2,128)S(1)}) custom-call(bf16[1,2,256,2048]{3,2,1,0:T(8,128)(2,1)} %facets.1, f32[16,2,512]{2,1,0:T(2,128)S(1)} %copy-done, s32[4,32]{1,0:T(4,128)S(1)} %pad_add_fusion.offsets_in), custom_call_target="tpu_custom_call" | custom-call | flops 3000000000 | bytes 4000000 | tf_op jit(solution)/shard_map/round_trip/pallas_call | solution.py:439
  55.6 1.7 %correction.1 = (bf16[1,2,256,2048]{3,2,1,0:T(8,128)(2,1)}, f32[16,2,2,512]{3,2,1,0:T(2,128)}) custom-call(bf16[256,256]{1,0:T(8,128)(2,1)S(1)} %get-tuple-element.5.et, bf16[256,2048]{1,0:T(8,128)(2,1)S(1)} %get-tuple-element.6.q, f32[16,2,2,512]{3,2,1,0:T(2,128)S(1)} %get-tuple-element.7.spectra_in), custom_call_target="tpu_custom_call" | custom-call | flops 1000000000 | bytes 3000000 | tf_op jit(solution)/shard_map/correction/pallas_call | solution.py:490
Async XLA Ops:
  2.0 0.8 %copy-start = (f32[16,2,512]{2,1,0:T(2,128)S(1)}, f32[16,2,512]{2,1,0:T(2,128)}, u32[]{:S(2)}) copy-start(f32[16,2,512]{2,1,0:T(2,128)} %weights.1) | copy-start | bytes 196612

commit v8 on v7

--- a/solution.py
+++ b/solution.py
@@ -261,14 +261,10 @@
 
     def to_all(action, first=1):
         for dc in (first, 1 - first):
-
-            @pl.loop(0, 7 + dc)
-            def _(i):
+            for i in range(8):
                 for dy in (1, 0):
-                    action(peer(i, dy, dc))
-
-            if dc == 0:
-                action(peer(7, 1, 0))
+                    if dc or dy or i < 7:
+                        action(peer(jnp.int32(i), dy, dc))
 
     for l in range(PAIR):
         low_k, high_k = own[l]

time: 57.4 us -> 57.4 us (level)
  no operation moved by 1% of the time
where the time goes in v8:
time: 57.4 us; the launch traced here: 57.3 us
  Pallas kernels  54.4 us (95%)
  between operations  1.29 us (2%)
  local copies, waits for them, and re-layouts  0.84 us (1%)
  other arithmetic  0.71 us (1%)
    pallas_call x1, Pallas kernels, shards(): pl.pallas_call(round_trip, out_shape=(jax.ShapeDtypeStruct((2 * M, ROWS),...  52.8 us
    pallas_call x1, Pallas kernels, shards(): pl.pallas_call(correction, out_shape=(jax.ShapeDtypeStruct((1, 2, ROWS, Y...  1.68 us

profile of v8, /device:TPU:1, one launch (start us, length us, event | category | flops | bytes accessed | tf_op | source)
XLA Modules:
  0.0 57.3 jit_solution(3713029451041818094)
XLA Ops:
  1.3 0.7 %pad_add_fusion.offsets_in = s32[4,32]{1,0:T(4,128)S(1)} fusion(s32[1,1]{1,0:T(1,128)} %bitcast.3, s32[1,16]{1,0:T(1,128)} %bitcast.5, s32[2,32]{1,0:T(2,128)} %bitcast.4), kind=kLoop, calls=%fused_computation | loop fusion | flops 256 | bytes 836 | tf_op jit(solution)/shard_map/add | solution.py:431
  2.0 0.0 copy-start
  2.0 0.8 %copy-done = f32[16,2,512]{2,1,0:T(2,128)S(1)} copy-done((f32[16,2,512]{2,1,0:T(2,128)S(1)}, f32[16,2,512]{2,1,0:T(2,128)}, u32[]{:S(2)}) %copy-start) | copy-done | bytes 65560
  2.8 52.8 %round_trip.1 = (bf16[256,256]{1,0:T(8,128)(2,1)S(1)}, bf16[256,2048]{1,0:T(8,128)(2,1)S(1)}, f32[16,2,2,512]{3,2,1,0:T(2,128)S(1)}) custom-call(bf16[1,2,256,2048]{3,2,1,0:T(8,128)(2,1)} %facets.1, f32[16,2,512]{2,1,0:T(2,128)S(1)} %copy-done, s32[4,32]{1,0:T(4,128)S(1)} %pad_add_fusion.offsets_in), custom_call_target="tpu_custom_call" | custom-call | flops 3000000000 | bytes 4000000 | tf_op jit(solution)/shard_map/round_trip/pallas_call | solution.py:435
  55.6 1.7 %correction.1 = (bf16[1,2,256,2048]{3,2,1,0:T(8,128)(2,1)}, f32[16,2,2,512]{3,2,1,0:T(2,128)}) custom-call(bf16[256,256]{1,0:T(8,128)(2,1)S(1)} %get-tuple-element.5.et, bf16[256,2048]{1,0:T(8,128)(2,1)S(1)} %get-tuple-element.6.q, f32[16,2,2,512]{3,2,1,0:T(2,128)S(1)} %get-tuple-element.7.spectra_in), custom_call_target="tpu_custom_call" | custom-call | flops 1000000000 | bytes 3000000 | tf_op jit(solution)/shard_map/correction/pallas_call | solution.py:486
Async XLA Ops:
  2.0 0.8 %copy-start = (f32[16,2,512]{2,1,0:T(2,128)S(1)}, f32[16,2,512]{2,1,0:T(2,128)}, u32[]{:S(2)}) copy-start(f32[16,2,512]{2,1,0:T(2,128)} %weights.1) | copy-start | bytes 196612
